TPU v7x, 128 devices: a whole 4x4x4 slice. The times are simulated.
128 devices in a mesh: expert: 128 (over x, z, y, core).
Axes of the slice: x: 4, y: 4, z: 4, core: 2. Of those that a mesh axis runs over, the one named last changes fastest.
Arguments:
- tokens: bfloat16 [8192, 2048], P('expert'), may hold values from -6 to 6
- expert_ids: int32 [8192, 8], P('expert'), may hold values from 0 to 127, as said below
- gate_scores: float32 [8192, 8], P('expert'), may hold values from 0.1 to 1
- w_gate: bfloat16 [128, 2048, 768], P('expert'), may hold values from -0.125 to 0.125
- w_up: bfloat16 [128, 2048, 768], P('expert'), may hold values from -0.125 to 0.125
- w_down: bfloat16 [128, 768, 2048], P('expert'), may hold values from -0.21875 to 0.21875
Outputs:
- mixed: bfloat16 [8192, 2048], P('expert')
Inputs may be any that keep to these rules, and one draw needn't show every extreme that they name: `expert_ids`: each row names 8 different experts. One set of 3 experts, the same everywhere, each is named by exactly 18 rows of each device's block of 64 rows; each other expert is named by at most 4 rows of one device's block, and some expert reaches 4 in every block.
All inputs are finite; a program needn't handle non-finite values.
Results may differ from a plain program's by a relative error of at most 0.0058.
Values may be sent and summed in bfloat16 or wider, within the bound.
No kernel may reach another device: no remote copies, remote signals or barrier semaphores. Data moves between devices by JAX's collectives and lax.ppermute only.
A program may use at most 192 MiB of HBM per device.

v0:
```python
import functools

import jax
import jax.numpy as jnp
from jax import lax
from jax.experimental import pallas as pl
from jax.experimental.pallas import tpu as pltpu
from jax.sharding import PartitionSpec as P

MOST = 18
BASE = 4
SPARE = 2
CAP = BASE + SPARE
HOT = 3
LINES = 16
DIRS = ((0, 1), (0, -1), (1, 1), (1, -1), (2, 1), (2, -1))
F32 = jnp.float32
BF16 = jnp.bfloat16


def split_index(i):
    return (i >> 5) & 3, (i >> 3) & 3, (i >> 1) & 3


def moved_chip(i, axis, step):
    c = list(split_index(i))
    c[axis] = (c[axis] + step) & 3
    return (c[0] * 4 + c[1]) * 4 + c[2]


def hop_pairs(axis, step, n):
    return [(i, moved_chip(i, axis, step) * 2 + (i & 1)) for i in range(n)]


def plan_kernel(me_ref, ids_ref, tok_ref, base_ref, spare_ref, slot_ref, meta_ref):
    rows, picks = ids_ref.shape
    n = 128
    me = me_ref[0]
    lane = lax.broadcasted_iota(jnp.int32, (1, n), 1)
    lower = (
        lax.broadcasted_iota(jnp.int32, (rows, rows), 1)
        < lax.broadcasted_iota(jnp.int32, (rows, rows), 0)
    ).astype(BF16)
    upper = (
        lax.broadcasted_iota(jnp.int32, (n, n), 0) < lax.broadcasted_iota(jnp.int32, (n, n), 1)
    ).astype(BF16)

    def before_lane(flags):
        wide = jnp.broadcast_to(flags, (8, n)).astype(BF16)
        return jnp.dot(wide, upper, preferred_element_type=F32)[0:1]

    ids = ids_ref[...]
    lane_rows = lax.broadcasted_iota(jnp.int32, (rows, n), 1)
    run = jnp.zeros((1, n), F32)
    ranks, members = [], []
    for k in range(picks):
        member = (ids[:, k : k + 1] == lane_rows).astype(F32)
        ahead = jnp.dot(lower, member.astype(BF16), preferred_element_type=F32) + run
        ranks.append(jnp.sum(ahead * member, axis=1, keepdims=True).astype(jnp.int32))
        members.append(member)
        run = run + jnp.sum(member, axis=0, keepdims=True)
    hot = (run > BASE + 0.5).astype(F32)
    hot_rank = before_lane(hot)

    chips, near, same = [], [], []
    dev = split_index(lane)
    for h in range(HOT):
        mine = hot * (hot_rank == float(h)).astype(F32)
        where_hot = jnp.sum(lane.astype(F32) * mine, axis=1, keepdims=True).astype(jnp.int32)
        chips.append(where_hot >> 1)
        dist = jnp.zeros((1, n), jnp.int32)
        for a, b in zip(dev, split_index(where_hot)):
            gap = (a - b) & 3
            dist = dist + jnp.minimum(gap, 4 - gap)
        same.append((dist == 0).astype(F32))
        near.append((dist == 1).astype(F32))
    taken = jnp.minimum(same[0] + same[1] + same[2], 1.0)
    near = [v * (1.0 - taken) for v in near]
    avail, slot_of, order = [], [], []
    used = jnp.zeros((1, n), F32)
    ok = jnp.ones((1, 1), F32)
    for h in range(HOT):
        free = near[h] * (used < SPARE - 0.5).astype(F32)
        avail.append(free)
        slot_of.append(used)
        order.append(before_lane(free))
        used = used + free
        enough = jnp.sum(free, axis=1, keepdims=True) > MOST - CAP - SPARE - 0.5
        ok = ok * enough.astype(F32)
    for a, b in ((0, 1), (0, 2), (1, 2)):
        ok = ok * (chips[a] != chips[b]).astype(F32)

    base_wide = lax.broadcasted_iota(jnp.int32, (rows, n * BASE), 1)
    spare_wide = lax.broadcasted_iota(jnp.int32, (rows, n * SPARE), 1)
    lane_f = lane.astype(F32)
    chosen_base = jnp.zeros(base_wide.shape, F32)
    chosen_spare = jnp.zeros(spare_wide.shape, F32)
    slot_cols = []
    for k in range(picks):
        e, q, member = ids[:, k : k + 1], ranks[k], members[k]
        which = jnp.sum(member * (hot * (hot_rank + 1.0)), axis=1, keepdims=True)
        code = jnp.where(q < CAP, e * 8 + q, (e ^ 1) * 8 + BASE + (q - CAP))
        far = jnp.zeros((rows, 1), F32)
        turn = (q - (CAP + SPARE)).astype(F32)
        for h in range(HOT):
            hit = avail[h] * (order[h] == turn).astype(F32) * (which == h + 1.0).astype(F32)
            far = far + jnp.sum(hit * (lane_f * 8 + BASE + slot_of[h]), axis=1, keepdims=True)
        code = jnp.where(q < CAP + SPARE, code, far.astype(jnp.int32))
        slot_cols.append(code)
        place, turn = code >> 3, code & 7
        at = jnp.where(turn < BASE, place * BASE + turn, -1)
        chosen_base = chosen_base + (at == base_wide).astype(F32)
        at = jnp.where(turn < BASE, -1, place * SPARE + turn - BASE)
        chosen_spare = chosen_spare + (at == spare_wide).astype(F32)
    slot_ref[...] = jnp.concatenate(slot_cols, axis=1)
    for chosen, out_ref in ((chosen_spare, spare_ref), (chosen_base, base_ref)):
        picked = lax.dot_general(
            chosen.astype(BF16), tok_ref[...], (((0,), (0,)), ((), ())),
            preferred_element_type=F32,
        )
        out_ref[...] = picked.astype(BF16).reshape(out_ref.shape)

    here = (lane == me).astype(F32)
    meta = jnp.zeros((1, n), F32)
    source = [jnp.zeros((1, n), F32) for _ in range(SPARE)]
    for d, (axis, step) in enumerate(DIRS):
        target = moved_chip(lane, axis, step)
        sent = jnp.zeros((1, n), F32)
        for h in range(HOT):
            serves = avail[h] * (target == chips[h]).astype(F32)
            sent = sent + serves * slot_of[h]
            for j in range(SPARE):
                source[j] = source[j] + serves * (slot_of[h] == float(j)).astype(F32) * (1.0 + d)
        meta = jnp.where(lane == d, jnp.sum(sent * here, axis=1, keepdims=True), meta)
    for j in range(SPARE):
        meta = jnp.where(lane == 6 + j, jnp.sum(source[j] * here, axis=1, keepdims=True), meta)
    meta = jnp.where(lane == 8, jnp.sum(hot * here, axis=1, keepdims=True), meta)
    meta = jnp.where(lane == 9, jnp.sum(taken * here, axis=1, keepdims=True), meta)
    meta = jnp.where(lane == 10, ok, meta)
    meta_ref[...] = meta.astype(jnp.int32)


def plan(me, ids, tokens):
    rows, width = tokens.shape
    vmem = pl.BlockSpec(memory_space=pltpu.VMEM)
    return pl.pallas_call(
        plan_kernel,
        in_specs=[pl.BlockSpec(memory_space=pltpu.SMEM), vmem, vmem],
        out_specs=[vmem] * 4,
        out_shape=[
            jax.ShapeDtypeStruct((128, BASE, width), BF16),
            jax.ShapeDtypeStruct((128, SPARE, width), BF16),
            jax.ShapeDtypeStruct(ids.shape, jnp.int32),
            jax.ShapeDtypeStruct((1, 128), jnp.int32),
        ],
        compiler_params=pltpu.CompilerParams(vmem_limit_bytes=24 * 2**20),
        name="plan",
    )(me, ids, tokens)


VMEM = pl.BlockSpec(memory_space=pltpu.VMEM)
SMEM = pl.BlockSpec(memory_space=pltpu.SMEM)
HBM = pl.BlockSpec(memory_space=pltpu.HBM)
BLOCK = 256


def spread_kernel(flags_ref, got_ref, *refs):
    outs, parts_ref, sems = refs[:-2], refs[-2], refs[-1]
    n, spare, width = got_ref.shape
    got = got_ref[...].reshape(n * spare, width)
    row = lax.broadcasted_iota(jnp.int32, (n, n * spare), 0)
    column = lax.broadcasted_iota(jnp.int32, (n, n * spare), 1)
    for s in range(SPARE):
        take = (row * spare + s == column).astype(BF16)
        parts_ref[s] = jnp.dot(take, got, preferred_element_type=F32).astype(BF16)
    copies = [
        pltpu.make_async_copy(parts_ref.at[i if i < SPARE else flags_ref[i - SPARE]], out, sems.at[i])
        for i, out in enumerate(outs)
    ]
    for copy in copies:
        copy.start()
    for copy in copies:
        copy.wait()


def spread(flags, got):
    n, spare, width = got.shape
    count = SPARE + len(DIRS)
    return pl.pallas_call(
        spread_kernel,
        in_specs=[SMEM, VMEM],
        out_specs=[HBM] * count,
        out_shape=[jax.ShapeDtypeStruct((n, width), BF16)] * count,
        scratch_shapes=[pltpu.VMEM((SPARE, n, width), BF16), pltpu.SemaphoreType.DMA((count,))],
        compiler_params=pltpu.CompilerParams(vmem_limit_bytes=24 * 2**20),
        name="spread",
    )(flags, got)


PANEL = 512


def fetch(weights, scratch):
    gate, up, down = weights
    hid_ref, gate_ref, up_ref, down_ref, sems = scratch
    blocks, panels = gate_ref.shape[0], down_ref.shape[0]
    for p in range(blocks):
        at = pl.ds(p * BLOCK, BLOCK)
        pltpu.make_async_copy(gate.at[0, :, at], gate_ref.at[p], sems.at[2 * p]).start()
        pltpu.make_async_copy(up.at[0, :, at], up_ref.at[p], sems.at[2 * p + 1]).start()
    for c in range(panels):
        at = pl.ds(c * PANEL, PANEL)
        pltpu.make_async_copy(down.at[0, :, at], down_ref.at[c], sems.at[2 * blocks + c]).start()


def ffn_rows(x_ref, out_ref, scratch):
    hid_ref, gate_ref, up_ref, down_ref, sems = scratch
    blocks, panels = gate_ref.shape[0], down_ref.shape[0]

    @pl.loop(0, blocks)
    def _(p):
        pltpu.make_async_copy(gate_ref.at[p], gate_ref.at[p], sems.at[2 * p]).wait()
        pltpu.make_async_copy(up_ref.at[p], up_ref.at[p], sems.at[2 * p + 1]).wait()
        x = x_ref[...]
        gate_act = jnp.dot(x, gate_ref[p], preferred_element_type=F32)
        upper = jnp.dot(x, up_ref[p], preferred_element_type=F32)
        hid_ref[p] = (jax.nn.silu(gate_act) * upper).astype(BF16)

    @pl.loop(0, panels)
    def _(c):
        pltpu.make_async_copy(down_ref.at[c], down_ref.at[c], sems.at[2 * blocks + c]).wait()
        part = jnp.dot(hid_ref[0], down_ref[c, :BLOCK], preferred_element_type=F32)
        for p in range(1, blocks):
            part += jnp.dot(
                hid_ref[p], down_ref[c, p * BLOCK : (p + 1) * BLOCK], preferred_element_type=F32
            )
        out_ref[:, pl.ds(pl.multiple_of(c * PANEL, PANEL), PANEL)] = part.astype(BF16)


def ffn_scratch(rows, width, inner, more=0):
    blocks, panels = inner // BLOCK, width // PANEL
    return [
        pltpu.VMEM((blocks, rows, BLOCK), BF16),
        pltpu.VMEM((blocks, width, BLOCK), BF16),
        pltpu.VMEM((blocks, width, BLOCK), BF16),
        pltpu.VMEM((panels, inner, PANEL), BF16),
        pltpu.SemaphoreType.DMA((2 * blocks + panels + more,)),
    ]


def ffn_cost(rows, width, inner):
    return pl.CostEstimate(
        flops=6 * rows * width * inner, bytes_accessed=6 * width * inner, transcendentals=0
    )


def ffn_kernel(x_ref, gate, up, down, out_ref, rows_ref, *scratch):
    fetch((gate, up, down), scratch)
    rows_ref[...] = x_ref[...].reshape(rows_ref.shape)
    ffn_rows(rows_ref, out_ref, scratch)


def ffn(x, gate_mat, up_mat, down_mat):
    n, slots, width = x.shape
    inner = gate_mat.shape[2]
    rows = n * slots
    return pl.pallas_call(
        ffn_kernel,
        in_specs=[VMEM] + [HBM] * 3,
        out_specs=VMEM,
        out_shape=jax.ShapeDtypeStruct((rows, width), BF16),
        scratch_shapes=[pltpu.VMEM((rows, width), BF16)] + ffn_scratch(rows, width, inner),
        compiler_params=pltpu.CompilerParams(vmem_limit_bytes=40 * 2**20),
        cost_estimate=ffn_cost(rows, width, inner),
        name="ffn",
    )(x, gate_mat, up_mat, down_mat)


def hot_kernel(groups, flags_ref, *refs):
    xs, refs = refs[:groups], refs[groups:]
    own, other, refs = refs[:3], refs[3:6], refs[6:]
    outs, (rows_ref, done_ref, *scratch) = refs[:groups], refs[groups:]
    n = xs[0].shape[0]
    sems = scratch[-1]
    base = sems.shape[0] - groups

    @pl.when(flags_ref[9] == 1)
    def _():
        parts = [pl.ds(g * n, n) for g in range(groups)]
        arriving = [
            pltpu.make_async_copy(x, rows_ref.at[at], sems.at[base + g])
            for g, (x, at) in enumerate(zip(xs, parts))
        ]
        for copy in arriving:
            copy.start()

        @pl.when(flags_ref[8] == 1)
        def _():
            fetch(own, scratch)

        @pl.when(flags_ref[8] == 0)
        def _():
            fetch(other, scratch)

        for copy in arriving:
            copy.wait()
        ffn_rows(rows_ref, done_ref, scratch)
        leaving = [
            pltpu.make_async_copy(done_ref.at[at], out, sems.at[base + g])
            for g, (out, at) in enumerate(zip(outs, parts))
        ]
        for copy in leaving:
            copy.start()
        for copy in leaving:
            copy.wait()


def hot_ffn(flags, xs, own, other):
    n, width = xs[0].shape
    inner = own[0].shape[2]
    rows = n * len(xs)
    return pl.pallas_call(
        functools.partial(hot_kernel, len(xs)),
        in_specs=[SMEM] + [HBM] * (len(xs) + 6),
        out_specs=[HBM] * len(xs),
        out_shape=[jax.ShapeDtypeStruct((n, width), BF16)] * len(xs),
        scratch_shapes=[pltpu.VMEM((rows, width), BF16)] * 2
        + ffn_scratch(rows, width, inner, len(xs)),
        compiler_params=pltpu.CompilerParams(vmem_limit_bytes=60 * 2**20),
        cost_estimate=ffn_cost(rows, width, inner),
        name="hot_ffn",
    )(flags, *xs, *own, *other)


def join_kernel(flags_ref, served_ref, *refs):
    own, back = refs[:SPARE], refs[SPARE : SPARE + len(DIRS)]
    out_ref, pick_ref, sems = refs[SPARE + len(DIRS) :]
    n, lines, _ = out_ref.shape
    width = served_ref.shape[1]
    half = width // 2
    for s in range(SPARE):
        at = pl.ds(2 * s * n, 2 * n)

        @pl.when((flags_ref[6 + s] == 0) & (flags_ref[9] == 0))
        def _():
            pick_ref[at, :] = jnp.zeros((2 * n, half), BF16)

        for d, source in enumerate((own[s],) + back):
            @pl.when((flags_ref[6 + s] == d) & ((d > 0) | (flags_ref[9] == 1)))
            def _():
                copies = [
                    pltpu.make_async_copy(
                        source.at[:, pl.ds(t * half, half)],
                        pick_ref.at[pl.ds((2 * s + t) * n, n)],
                        sems.at[t],
                    )
                    for t in range(2)
                ]
                for copy in copies:
                    copy.start()
                for copy in copies:
                    copy.wait()

    out_ref[:, :, :width] = served_ref[...].reshape(n, lines, width)
    row = lax.broadcasted_iota(jnp.int32, (n * lines, lines * n), 0)
    column = lax.broadcasted_iota(jnp.int32, (n * lines, lines * n), 1)
    put = ((row & (lines - 1)) * n + row // lines == column).astype(BF16)
    placed = jnp.dot(put, pick_ref[...], preferred_element_type=F32)
    out_ref[:, :, width:] = placed.astype(BF16).reshape(n, lines, half)


def join(flags, served, own, back):
    n, width = own[0].shape
    return pl.pallas_call(
        join_kernel,
        in_specs=[SMEM, VMEM] + [HBM] * (SPARE + len(DIRS)),
        out_specs=VMEM,
        out_shape=jax.ShapeDtypeStruct((n, BASE, width * CAP // BASE), BF16),
        scratch_shapes=[pltpu.VMEM((n * BASE, width // 2), BF16), pltpu.SemaphoreType.DMA((2,))],
        compiler_params=pltpu.CompilerParams(vmem_limit_bytes=24 * 2**20),
        name="join",
    )(flags, served, *own, *back)


def mix_kernel(score_ref, slot_ref, ans_ref, out_ref):
    rows, picks = slot_ref.shape
    n, lines, _ = ans_ref.shape
    width = out_ref.shape[1]
    half = width // 2
    scores = score_ref[...]
    weights = scores / jnp.sum(scores, axis=1, keepdims=True)
    slots = slot_ref[...]
    place, turn = slots >> 3, slots & 7
    base = jnp.where(turn < BASE, place * lines + turn, -2)
    spare = jnp.where(turn < BASE, -2, place * lines + 2 * (turn - BASE))

    def spread_weights(at):
        wide = lax.broadcasted_iota(jnp.int32, (rows, n * lines), 1)
        full = jnp.zeros(wide.shape, F32)
        for k in range(picks):
            full = jnp.where(at[:, k : k + 1] == wide, weights[:, k : k + 1], full)
        high = full.astype(BF16)
        low = (full - high.astype(F32)).astype(BF16)
        return jnp.concatenate([high, low], axis=0)

    base_mix = spread_weights(base)
    answers = ans_ref[:, :, :width].reshape(n * lines, width)
    extra = ans_ref[:, :, width:].reshape(n * lines, half)
    for t in range(2):
        at = slice(t * half, (t + 1) * half)
        part = jnp.dot(base_mix, answers[:, at], preferred_element_type=F32)
        part += jnp.dot(spread_weights(spare + t), extra, preferred_element_type=F32)
        out_ref[:, at] = (part[:rows] + part[rows:]).astype(BF16)


def mix(scores, slots, answers):
    n, lines, wide = answers.shape
    return pl.pallas_call(
        mix_kernel,
        in_specs=[VMEM] * 3,
        out_specs=VMEM,
        out_shape=jax.ShapeDtypeStruct((slots.shape[0], wide * BASE // CAP), BF16),
        compiler_params=pltpu.CompilerParams(vmem_limit_bytes=24 * 2**20),
        name="mix",
    )(scores, slots, answers)


def exchange(x):
    return lax.all_to_all(x, "expert", split_axis=0, concat_axis=0, tiled=True)


def relayed(scores, w_gate, w_up, w_down, base, spare, slots, meta):
    n = lax.axis_size("expert")
    flags = meta[0]
    swap = [(i, i ^ 1) for i in range(n)]
    own = (w_gate, w_up, w_down)
    other = [lax.ppermute(w, "expert", swap) for w in own]
    got_spare, base, *other = lax.optimization_barrier((exchange(spare), base, *other))
    got_base = exchange(base)
    parts = spread(flags, got_spare)
    kept, sent = parts[:SPARE], parts[SPARE:]
    hopped = [
        lax.ppermute(x, "expert", hop_pairs(axis, step, n)) for x, (axis, step) in zip(sent, DIRS)
    ]
    first = hot_ffn(flags, kept, own, other)
    first, early = lax.optimization_barrier((first, hopped[:3]))
    second = hot_ffn(flags, early, own, other)
    third = hot_ffn(flags, hopped[3:], own, other)
    back = [
        lax.ppermute(x, "expert", hop_pairs(axis, -step, n))
        for x, (axis, step) in zip(list(second) + list(third), DIRS)
    ]
    got_base, *_ = lax.optimization_barrier((got_base, *third))
    served = ffn(got_base, *own)
    return mix(scores, slots, exchange(join(flags, served, first, back)))


def expert_ffn(rows, gate_mat, up_mat, down_mat):
    gate_act = jnp.dot(rows, gate_mat, preferred_element_type=F32)
    upper = jnp.dot(rows, up_mat, preferred_element_type=F32)
    hidden = (jax.nn.silu(gate_act) * upper).astype(BF16)
    return jnp.dot(hidden, down_mat, preferred_element_type=F32).astype(BF16)


def direct(tokens, ids, scores, w_gate, w_up, w_down):
    rows, picks = ids.shape
    n = lax.axis_size("expert")
    width = tokens.shape[1]
    weights = scores / jnp.sum(scores, axis=1, keepdims=True)
    flat = ids.reshape(-1)
    experts = jnp.arange(n, dtype=jnp.int32)
    member = (flat[:, None] == experts[None, :]).astype(jnp.int32)
    before = jnp.cumsum(member, axis=0) - member
    target = flat * MOST + jnp.sum(before * member, axis=1)
    sent = jnp.zeros((n * MOST, width), BF16).at[target].set(jnp.repeat(tokens, picks, axis=0))
    got = exchange(sent.reshape(n, MOST * LINES, 128))
    served = expert_ffn(got.reshape(n * MOST, width), w_gate[0], w_up[0], w_down[0])
    answered = exchange(served.reshape(n, MOST * LINES, 128)).reshape(n * MOST, width)
    picked = weights.reshape(-1)[:, None] * answered[target].astype(F32)
    return jnp.sum(picked.reshape(rows, picks, width), axis=1).astype(BF16)


def body(tokens, ids, scores, w_gate, w_up, w_down):
    me = lax.axis_index("expert").astype(jnp.int32).reshape(1)
    base, spare, slots, meta = plan(me, ids, tokens)
    mixed = relayed(scores, w_gate, w_up, w_down, base, spare, slots, meta)
    return lax.cond(
        meta[0, 10] == 1,
        lambda mixed, *rest: mixed,
        lambda mixed, *rest: direct(*rest),
        mixed, tokens, ids, scores, w_gate, w_up, w_down,
    )


def solution(mesh):
    placed = (
        P("expert", None),
        P("expert", None),
        P("expert", None),
        P("expert", None, None),
        P("expert", None, None),
        P("expert", None, None),
    )
    return jax.shard_map(
        body, mesh=mesh, in_specs=placed, out_specs=P("expert", None), check_vma=False
    )
```

profile of v0, /device:TPU:1, one launch (start us, length us, event | category | flops | bytes accessed | tf_op | source)
XLA Modules:
  0.0 172.3 jit_solution(2477275398981223211)
XLA Ops:
  0.0 1.4 collective-permute-start
  2.7 4.3 %plan.1 = (bf16[128,4,2048]{2,1,0:T(4,128)(2,1)}, bf16[128,2,2048]{2,1,0:T(2,128)(2,1)S(1)}, s32[64,8]{1,0:T(8,128)S(1)}, s32[1,128]{1,0:T(1,128)S(1)}) custom-call(s32[1]{0:T(128)} %bitcast.10.me_ref, s32[64,8]{1,0:T(8,128)S(1)} %copy.14.ids_ref, bf16[64,2048]{1,0:T(8,128)(2,1)} %tok_ref.1), custom_call_target="tpu_custom_call" | custom-call | tf_op jit(solution)/shard_map/plan/pallas_call | solution.py:146
  7.0 29.1 %all_to_all.24.got_ref = bf16[128,2,2048]{2,1,0:T(2,128)(2,1)S(1)} all-to-all(bf16[128,2,2048]{2,1,0:T(2,128)(2,1)S(1)} %get-tuple-element.60), channel_id=1, replica_groups=mesh['expert'=128] {'expert'}, dimensions={0} | all-to-all | bytes 2097152 | tf_op jit(solution)/shard_map/all_to_all | solution.py:429
  36.1 4.7 %all-to-all-start.3 = ((bf16[128,4,2048]{2,1,0:T(4,128)(2,1)}), bf16[128,4,2048]{2,1,0:T(4,128)(2,1)S(1)}, u32[]{:S(2)}, u32[]{:S(2)}) async-start(bf16[128,4,2048]{2,1,0:T(4,128)(2,1)} %get-tuple-element.62), calls=%async_computation.3 | async-start | bytes 4194304 | tf_op jit(solution)/shard_map/all_to_all | solution.py:429
  40.8 2.7 %spread.1 = (bf16[128,2048]{1,0:T(8,128)(2,1)S(1)}, bf16[128,2048]{1,0:T(8,128)(2,1)S(1)}, bf16[128,2048]{1,0:T(8,128)(2,1)}, bf16[128,2048]{1,0:T(8,128)(2,1)},...) custom-call(s32[128]{0:T(128)S(1)} %bitcast.36, ...), custom_call_target="tpu_custom_call" | custom-call | tf_op jit(solution)/shard_map/spread/pallas_call | solution.py:189
  44.3 0.8 copy-done.6
  45.1 1.4 collective-permute-start.6
  46.5 1.3 collective-permute-start.7
  47.8 1.6 collective-permute-start.8
  49.4 1.8 %collective-permute-start.3 = (bf16[128,2048]{1,0:T(8,128)(2,1)}, bf16[128,2048]{1,0:T(8,128)(2,1)S(1)}, u32[]{:S(2)}, u32[]{:S(2)}) collective-permute-start(bf16[128,2048]{1,0:T(8,128)(2,1)} %get-tuple-element.64), channel_id=1, source_target_pairs={{0,24},{1,25},{2,26},{3,27},{4,28},{5,29},{6,30},{7,31},{8,0},{9,1... | collective-permute-start | bytes 1572872 | tf_op jit(solution)/shard_map/ppermute | solution.py:443
  51.1 1.2 collective-permute-start.4
  53.2 24.3 %collective-permute-done.6.refs_0_ = bf16[128,2048]{1,0:T(8,128)(2,1)} collective-permute-done((bf16[128,2048]{1,0:T(8,128)(2,1)}, bf16[128,2048]{1,0:T(8,128)(2,1)}, u32[]{:S(2)}, u32[]{:S(2)}) %collective-permute-start.6) | collective-permute-done | bytes 524320 | tf_op jit(solution)/shard_map/ppermute | solution.py:443
  77.5 2.4 %collective-permute-start.5 = (bf16[128,2048]{1,0:T(8,128)(2,1)}, bf16[128,2048]{1,0:T(8,128)(2,1)}, u32[]{:S(2)}, u32[]{:S(2)}) collective-permute-start(bf16[128,2048]{1,0:T(8,128)(2,1)} %get-tuple-element.66), channel_id=1, source_target_pairs={{0,6},{1,7},{2,0},{3,1},{4,2},{5,3},{6,4},{7,5},{8,14},{9,15},{10,... | collective-permute-start | bytes 1572872 | tf_op jit(solution)/shard_map/ppermute | solution.py:443
  81.1 11.2 %collective-permute-start.11 = (bf16[128,2048]{1,0:T(8,128)(2,1)}, bf16[128,2048]{1,0:T(8,128)(2,1)}, u32[]{:S(2)}, u32[]{:S(2)}) collective-permute-start(bf16[128,2048]{1,0:T(8,128)(2,1)} %get-tuple-element.88), channel_id=1, source_target_pairs={{0,24},{1,25},{2,26},{3,27},{4,28},{5,29},{6,30},{7,31},{8,0},{9,1... | collective-permute-start | bytes 1572872 | tf_op jit(solution)/shard_map/ppermute | solution.py:450
  92.3 2.6 %collective-permute-start.9 = (bf16[128,2048]{1,0:T(8,128)(2,1)}, bf16[128,2048]{1,0:T(8,128)(2,1)}, u32[]{:S(2)}, u32[]{:S(2)}) collective-permute-start(bf16[128,2048]{1,0:T(8,128)(2,1)} %get-tuple-element.86), channel_id=1, source_target_pairs={{0,96},{1,97},{2,98},{3,99},{4,100},{5,101},{6,102},{7,103},{8,104... | collective-permute-start | bytes 1572872 | tf_op jit(solution)/shard_map/ppermute | solution.py:450
  96.6 6.5 %collective-permute-start.13 = (bf16[128,2048]{1,0:T(8,128)(2,1)}, bf16[128,2048]{1,0:T(8,128)(2,1)}, u32[]{:S(2)}, u32[]{:S(2)}) collective-permute-start(bf16[128,2048]{1,0:T(8,128)(2,1)} %get-tuple-element.71), channel_id=1, source_target_pairs={{0,6},{1,7},{2,0},{3,1},{4,2},{5,3},{6,4},{7,5},{8,14},{9,15},{10,... | collective-permute-start | bytes 1572872 | tf_op jit(solution)/shard_map/ppermute | solution.py:450
  103.9 7.8 %ffn.1.served_ref = bf16[512,2048]{1,0:T(8,128)(2,1)S(1)} custom-call(bf16[128,4,2048]{2,1,0:T(4,128)(2,1)S(1)} %all-to-all-done.3.x_ref, bf16[1,2048,768]{2,1,0:T(8,128)(2,1)} %refs_3_.5, bf16[1,2048,768]{2,1,0:T(8,128)(2,1)} %refs_4_.5, bf16[1,768,2048]{2,1,0:T(8,128)(2,1)} %refs_5_.3), custom_call_target="tpu_custom_call" | custom-call | flops 4831838208 | bytes 9437184 | tf_op jit(solution)/shard_map/ffn/pallas_call | solution.py:267
  111.8 3.9 %collective-permute-done.12.refs_5_ = bf16[128,2048]{1,0:T(8,128)(2,1)} collective-permute-done((bf16[128,2048]{1,0:T(8,128)(2,1)}, bf16[128,2048]{1,0:T(8,128)(2,1)}, u32[]{:S(2)}, u32[]{:S(2)}) %collective-permute-start.12) | collective-permute-done | bytes 524320 | tf_op jit(solution)/shard_map/ppermute | solution.py:450
  115.7 1.2 collective-permute-done.14.refs_7_
  116.9 3.6 %join.1 = bf16[128,4,3072]{2,1,0:T(4,128)(2,1)S(1)} custom-call(s32[128]{0:T(128)S(1)} %bitcast.40, bf16[512,2048]{1,0:T(8,128)(2,1)S(1)} %ffn.1.served_ref, bf16[128,2048]{1,0:T(8,128)(2,1)S(1)} %copy-done.1, bf16[128,2048]{1,0:T(8,128)(2,1)S(1)} %copy-done.2, bf16[128,2048]{1,0:T(8,128)(2,1)} %collective-permute-done.9.refs_2_, ...), custom_call_target="tpu_custom_call" | custom-call | tf_op jit(solution)/shard_map/join/pallas_call | solution.py:374
  120.5 1.6 copy-done
  122.1 6.5 %all-to-all-start.4 = ((bf16[128,4,3072]{2,1,0:T(4,128)(2,1)}), bf16[128,4,3072]{2,1,0:T(4,128)(2,1)S(1)}, u32[]{:S(2)}, u32[]{:S(2)}) async-start(bf16[128,4,3072]{2,1,0:T(4,128)(2,1)} %copy-done), calls=%async_computation.4 | async-start | bytes 6291456 | tf_op jit(solution)/shard_map/all_to_all | solution.py:429
  129.9 40.5 %all-to-all-done.4.ans_ref = bf16[128,4,3072]{2,1,0:T(4,128)(2,1)S(1)} async-done(((bf16[128,4,3072]{2,1,0:T(4,128)(2,1)}), bf16[128,4,3072]{2,1,0:T(4,128)(2,1)S(1)}, u32[]{:S(2)}, u32[]{:S(2)}) %all-to-all-start.4) | async-done | bytes 3145760 | tf_op jit(solution)/shard_map/all_to_all | solution.py:429
  170.4 1.8 %mix.1 = bf16[64,2048]{1,0:T(8,128)(2,1)} custom-call(f32[64,8]{1,0:T(8,128)S(1)} %copy.15.score_ref, s32[64,8]{1,0:T(8,128)S(1)} %get-tuple-element.59.slot_ref, bf16[128,4,3072]{2,1,0:T(4,128)(2,1)S(1)} %all-to-all-done.4.ans_ref), custom_call_target="tpu_custom_call" | custom-call | tf_op jit(solution)/shard_map/mix/pallas_call | solution.py:418
  (51 shorter events, 7.3 us)
Async XLA Ops:
  0.0 36.1 %collective-permute-start = (bf16[1,2048,768]{2,1,0:T(8,128)(2,1)}, bf16[1,2048,768]{2,1,0:T(8,128)(2,1)}, u32[]{:S(2)}, u32[]{:S(2)}) collective-permute-start(bf16[1,2048,768]{2,1,0:T(8,128)(2,1)} %refs_3_.5), channel_id=1, source_target_pairs={{0,1},{1,0},{2,3},{3,2},{4,5},{5,4},{6,7},{7,6},{8,9},{9,8},{10,11... | collective-permute-start | bytes 9437192 | tf_op jit(solution)/shard_map/ppermute | solution.py:437
  1.4 34.7 %collective-permute-start.1 = (bf16[1,2048,768]{2,1,0:T(8,128)(2,1)}, bf16[1,2048,768]{2,1,0:T(8,128)(2,1)}, u32[]{:S(2)}, u32[]{:S(2)}) collective-permute-start(bf16[1,2048,768]{2,1,0:T(8,128)(2,1)} %refs_4_.5), channel_id=1, source_target_pairs={{0,1},{1,0},{2,3},{3,2},{4,5},{5,4},{6,7},{7,6},{8,9},{9,8},{10,11... | collective-permute-start | bytes 9437192 | tf_op jit(solution)/shard_map/ppermute | solution.py:437
  1.4 34.7 %collective-permute-start.2 = (bf16[1,768,2048]{2,1,0:T(8,128)(2,1)}, bf16[1,768,2048]{2,1,0:T(8,128)(2,1)}, u32[]{:S(2)}, u32[]{:S(2)}) collective-permute-start(bf16[1,768,2048]{2,1,0:T(8,128)(2,1)} %refs_5_.3), channel_id=1, source_target_pairs={{0,1},{1,0},{2,3},{3,2},{4,5},{5,4},{6,7},{7,6},{8,9},{9,8},{10,11... | collective-permute-start | bytes 9437192 | tf_op jit(solution)/shard_map/ppermute | solution.py:437
  7.0 45.4 %copy-start.7 = (s32[1,128]{1,0:T(1,128)}, s32[1,128]{1,0:T(1,128)S(1)}, u32[]{:S(2)}) copy-start(s32[1,128]{1,0:T(1,128)S(1)} %get-tuple-element.58) | copy-start | bytes 1540
  36.1 67.8 %all-to-all-start.3 = ((bf16[128,4,2048]{2,1,0:T(4,128)(2,1)}), bf16[128,4,2048]{2,1,0:T(4,128)(2,1)S(1)}, u32[]{:S(2)}, u32[]{:S(2)}) async-start(bf16[128,4,2048]{2,1,0:T(4,128)(2,1)} %get-tuple-element.62), calls=%async_computation.3 | async-start | bytes 4194304 | tf_op jit(solution)/shard_map/all_to_all | solution.py:429
  45.1 32.3 %collective-permute-start.6 = (bf16[128,2048]{1,0:T(8,128)(2,1)}, bf16[128,2048]{1,0:T(8,128)(2,1)}, u32[]{:S(2)}, u32[]{:S(2)}) collective-permute-start(bf16[128,2048]{1,0:T(8,128)(2,1)} %get-tuple-element.78), channel_id=1, source_target_pairs={{0,32},{1,33},{2,34},{3,35},{4,36},{5,37},{6,38},{7,39},{8,40},{9,... | collective-permute-start | bytes 1572872 | tf_op jit(solution)/shard_map/ppermute | solution.py:443
  46.5 33.4 %collective-permute-start.7 = (bf16[128,2048]{1,0:T(8,128)(2,1)}, bf16[128,2048]{1,0:T(8,128)(2,1)}, u32[]{:S(2)}, u32[]{:S(2)}) collective-permute-start(bf16[128,2048]{1,0:T(8,128)(2,1)} %get-tuple-element.79), channel_id=1, source_target_pairs={{0,96},{1,97},{2,98},{3,99},{4,100},{5,101},{6,102},{7,103},{8,104... | collective-permute-start | bytes 1572872 | tf_op jit(solution)/shard_map/ppermute | solution.py:443
  47.8 32.1 %collective-permute-start.8 = (bf16[128,2048]{1,0:T(8,128)(2,1)S(1)}, bf16[128,2048]{1,0:T(8,128)(2,1)}, u32[]{:S(2)}, u32[]{:S(2)}) collective-permute-start(bf16[128,2048]{1,0:T(8,128)(2,1)S(1)} %get-tuple-element.80), channel_id=1, source_target_pairs={{0,8},{1,9},{2,10},{3,11},{4,12},{5,13},{6,14},{7,15},{8,16},{9,17... | collective-permute-start | bytes 1572872 | tf_op jit(solution)/shard_map/ppermute | solution.py:443
  49.4 42.9 %collective-permute-start.3 = (bf16[128,2048]{1,0:T(8,128)(2,1)}, bf16[128,2048]{1,0:T(8,128)(2,1)S(1)}, u32[]{:S(2)}, u32[]{:S(2)}) collective-permute-start(bf16[128,2048]{1,0:T(8,128)(2,1)} %get-tuple-element.64), channel_id=1, source_target_pairs={{0,24},{1,25},{2,26},{3,27},{4,28},{5,29},{6,30},{7,31},{8,0},{9,1... | collective-permute-start | bytes 1572872 | tf_op jit(solution)/shard_map/ppermute | solution.py:443
  51.1 43.7 %collective-permute-start.4 = (bf16[128,2048]{1,0:T(8,128)(2,1)}, bf16[128,2048]{1,0:T(8,128)(2,1)S(1)}, u32[]{:S(2)}, u32[]{:S(2)}) collective-permute-start(bf16[128,2048]{1,0:T(8,128)(2,1)} %get-tuple-element.65), channel_id=1, source_target_pairs={{0,2},{1,3},{2,4},{3,5},{4,6},{5,7},{6,0},{7,1},{8,10},{9,11},{10,... | collective-permute-start | bytes 1572872 | tf_op jit(solution)/shard_map/ppermute | solution.py:443
  77.5 17.4 %collective-permute-start.5 = (bf16[128,2048]{1,0:T(8,128)(2,1)}, bf16[128,2048]{1,0:T(8,128)(2,1)}, u32[]{:S(2)}, u32[]{:S(2)}) collective-permute-start(bf16[128,2048]{1,0:T(8,128)(2,1)} %get-tuple-element.66), channel_id=1, source_target_pairs={{0,6},{1,7},{2,0},{3,1},{4,2},{5,3},{6,4},{7,5},{8,14},{9,15},{10,... | collective-permute-start | bytes 1572872 | tf_op jit(solution)/shard_map/ppermute | solution.py:443
  80.7 22.4 %collective-permute-start.10 = (bf16[128,2048]{1,0:T(8,128)(2,1)}, bf16[128,2048]{1,0:T(8,128)(2,1)S(1)}, u32[]{:S(2)}, u32[]{:S(2)}) collective-permute-start(bf16[128,2048]{1,0:T(8,128)(2,1)} %get-tuple-element.87), channel_id=1, source_target_pairs={{0,32},{1,33},{2,34},{3,35},{4,36},{5,37},{6,38},{7,39},{8,40},{9,... | collective-permute-start | bytes 1572872 | tf_op jit(solution)/shard_map/ppermute | solution.py:450
  81.1 30.7 %collective-permute-start.11 = (bf16[128,2048]{1,0:T(8,128)(2,1)}, bf16[128,2048]{1,0:T(8,128)(2,1)}, u32[]{:S(2)}, u32[]{:S(2)}) collective-permute-start(bf16[128,2048]{1,0:T(8,128)(2,1)} %get-tuple-element.88), channel_id=1, source_target_pairs={{0,24},{1,25},{2,26},{3,27},{4,28},{5,29},{6,30},{7,31},{8,0},{9,1... | collective-permute-start | bytes 1572872 | tf_op jit(solution)/shard_map/ppermute | solution.py:450
  92.3 19.5 %collective-permute-start.9 = (bf16[128,2048]{1,0:T(8,128)(2,1)}, bf16[128,2048]{1,0:T(8,128)(2,1)}, u32[]{:S(2)}, u32[]{:S(2)}) collective-permute-start(bf16[128,2048]{1,0:T(8,128)(2,1)} %get-tuple-element.86), channel_id=1, source_target_pairs={{0,96},{1,97},{2,98},{3,99},{4,100},{5,101},{6,102},{7,103},{8,104... | collective-permute-start | bytes 1572872 | tf_op jit(solution)/shard_map/ppermute | solution.py:450
  96.5 19.2 %collective-permute-start.12 = (bf16[128,2048]{1,0:T(8,128)(2,1)}, bf16[128,2048]{1,0:T(8,128)(2,1)}, u32[]{:S(2)}, u32[]{:S(2)}) collective-permute-start(bf16[128,2048]{1,0:T(8,128)(2,1)} %get-tuple-element.70), channel_id=1, source_target_pairs={{0,8},{1,9},{2,10},{3,11},{4,12},{5,13},{6,14},{7,15},{8,16},{9,17... | collective-permute-start | bytes 1572872 | tf_op jit(solution)/shard_map/ppermute | solution.py:450
  96.6 19.1 %collective-permute-start.13 = (bf16[128,2048]{1,0:T(8,128)(2,1)}, bf16[128,2048]{1,0:T(8,128)(2,1)}, u32[]{:S(2)}, u32[]{:S(2)}) collective-permute-start(bf16[128,2048]{1,0:T(8,128)(2,1)} %get-tuple-element.71), channel_id=1, source_target_pairs={{0,6},{1,7},{2,0},{3,1},{4,2},{5,3},{6,4},{7,5},{8,14},{9,15},{10,... | collective-permute-start | bytes 1572872 | tf_op jit(solution)/shard_map/ppermute | solution.py:450
  103.9 13.0 %copy-start.1 = (bf16[128,2048]{1,0:T(8,128)(2,1)S(1)}, bf16[128,2048]{1,0:T(8,128)(2,1)}, u32[]{:S(2)}) copy-start(bf16[128,2048]{1,0:T(8,128)(2,1)} %get-tuple-element.81.refs_0_) | copy-start | bytes 1572868
  103.9 13.0 %copy-start.2 = (bf16[128,2048]{1,0:T(8,128)(2,1)S(1)}, bf16[128,2048]{1,0:T(8,128)(2,1)}, u32[]{:S(2)}) copy-start(bf16[128,2048]{1,0:T(8,128)(2,1)} %get-tuple-element.82.refs_1_) | copy-start | bytes 1572868
  103.9 13.0 %copy-start.8 = (s32[1,128]{1,0:T(1,128)S(1)}, s32[1,128]{1,0:T(1,128)}, u32[]{:S(2)}) copy-start(s32[1,128]{1,0:T(1,128)} %copy-done.7) | copy-start | bytes 1540
  103.9 13.0 %collective-permute-start.14 = (bf16[128,2048]{1,0:T(8,128)(2,1)}, bf16[128,2048]{1,0:T(8,128)(2,1)}, u32[]{:S(2)}, u32[]{:S(2)}) collective-permute-start(bf16[128,2048]{1,0:T(8,128)(2,1)} %get-tuple-element.72), channel_id=1, source_target_pairs={{0,2},{1,3},{2,4},{3,5},{4,6},{5,7},{6,0},{7,1},{8,10},{9,11},{10,... | collective-permute-start | bytes 1572872 | tf_op jit(solution)/shard_map/ppermute | solution.py:450
  103.9 13.0 %copy-start.4 = (bf16[128,2048]{1,0:T(8,128)(2,1)S(1)}, bf16[128,2048]{1,0:T(8,128)(2,1)}, u32[]{:S(2)}) copy-start(bf16[128,2048]{1,0:T(8,128)(2,1)} %copy-done.3) | copy-start | bytes 1572868
  122.1 50.2 %copy-start.10 = (bf16[64,2048]{1,0:T(8,128)(2,1)S(1)}, bf16[64,2048]{1,0:T(8,128)(2,1)}, u32[]{:S(2)}) copy-start(bf16[64,2048]{1,0:T(8,128)(2,1)} %tok_ref.1) | copy-start | bytes 786436
  122.1 50.2 %copy-start.14 = (s32[64,8]{0,1:T(8,128)S(1)}, s32[64,8]{0,1:T(8,128)}, u32[]{:S(2)}) copy-start(s32[64,8]{0,1:T(8,128)} %param.9) | copy-start | bytes 6148
  122.1 48.3 %all-to-all-start.4 = ((bf16[128,4,3072]{2,1,0:T(4,128)(2,1)}), bf16[128,4,3072]{2,1,0:T(4,128)(2,1)S(1)}, u32[]{:S(2)}, u32[]{:S(2)}) async-start(bf16[128,4,3072]{2,1,0:T(4,128)(2,1)} %copy-done), calls=%async_computation.4 | async-start | bytes 6291456 | tf_op jit(solution)/shard_map/all_to_all | solution.py:429
  (7 other events, 14.6 us)
where the time goes:
time: 173 us; the launch traced here: 172 us
  waiting for transfers between devices  69.9 us (40%)
  starting transfers between devices  43.5 us (25%)
  blocking collectives  29.1 us (17%)
  Pallas kernels  22.6 us (13%)
  local copies, waits for them, and re-layouts  6.32 us (4%)
    all_to_all x2, waiting for transfers between devices, exchange(): return lax.all_to_all(x, 'expert', split_axis=0, concat_axis=0, tiled=True)  40.5 us
    all_to_all x1, blocking collectives, exchange(): return lax.all_to_all(x, 'expert', split_axis=0, concat_axis=0, tiled=True)  29.1 us
    ppermute x6, waiting for transfers between devices, relayed(): lax.ppermute(x, 'expert', hop_pairs(axis, step, n))  24.3 us
    ppermute x6, starting transfers between devices, relayed(): lax.ppermute(x, 'expert', hop_pairs(axis, -step, n))  20.8 us
    all_to_all x2, starting transfers between devices, exchange(): return lax.all_to_all(x, 'expert', split_axis=0, concat_axis=0, tiled=True)  11.2 us
    ppermute x6, starting transfers between devices, relayed(): lax.ppermute(x, 'expert', hop_pairs(axis, step, n))  9.68 us
    pallas_call x1, Pallas kernels, ffn(): pl.pallas_call(ffn_kernel, in_specs=[VMEM] + [HBM] * 3, out_specs=VMEM, o...  7.84 us
    unnamed x30, local copies, waits for them, and re-layouts  5.74 us
  transfers between devices with their start and end apart: 17, of which 4 were waited for; matrix products, arithmetic and copies ran while one was open for 1% of the time, Pallas kernels for 10%

commit v1 on v0

--- a/solution.py
+++ b/solution.py
@@ -32,7 +32,7 @@
     return [(i, moved_chip(i, axis, step) * 2 + (i & 1)) for i in range(n)]
 
 
-def plan_kernel(me_ref, ids_ref, tok_ref, base_ref, spare_ref, slot_ref, meta_ref):
+def plan_kernel(me_ref, ids_ref, tok_ref, out_ref, slot_ref, meta_ref):
     rows, picks = ids_ref.shape
     n = 128
     me = me_ref[0]
@@ -90,11 +90,9 @@
     for a, b in ((0, 1), (0, 2), (1, 2)):
         ok = ok * (chips[a] != chips[b]).astype(F32)
 
-    base_wide = lax.broadcasted_iota(jnp.int32, (rows, n * BASE), 1)
-    spare_wide = lax.broadcasted_iota(jnp.int32, (rows, n * SPARE), 1)
+    wide = lax.broadcasted_iota(jnp.int32, (rows, n * BASE), 1)
     lane_f = lane.astype(F32)
-    chosen_base = jnp.zeros(base_wide.shape, F32)
-    chosen_spare = jnp.zeros(spare_wide.shape, F32)
+    chosen = [jnp.zeros(wide.shape, F32) for _ in range(3)]
     slot_cols = []
     for k in range(picks):
         e, q, member = ids[:, k : k + 1], ranks[k], members[k]
@@ -108,17 +106,23 @@
         code = jnp.where(q < CAP + SPARE, code, far.astype(jnp.int32))
         slot_cols.append(code)
         place, turn = code >> 3, code & 7
-        at = jnp.where(turn < BASE, place * BASE + turn, -1)
-        chosen_base = chosen_base + (at == base_wide).astype(F32)
-        at = jnp.where(turn < BASE, -1, place * SPARE + turn - BASE)
-        chosen_spare = chosen_spare + (at == spare_wide).astype(F32)
+        at = jnp.where(turn < BASE, place * BASE + turn, -2)
+        half_at = jnp.where(turn < BASE, -2, place * BASE + 2 * (turn - BASE))
+        for i, line in enumerate((at, half_at, half_at + 1)):
+            chosen[i] = chosen[i] + (line == wide).astype(F32)
     slot_ref[...] = jnp.concatenate(slot_cols, axis=1)
-    for chosen, out_ref in ((chosen_spare, spare_ref), (chosen_base, base_ref)):
-        picked = lax.dot_general(
-            chosen.astype(BF16), tok_ref[...], (((0,), (0,)), ((), ())),
+    width = tok_ref.shape[1]
+    half = width // 2
+
+    def take(picks_of, first, last):
+        return lax.dot_general(
+            picks_of.astype(BF16), tok_ref[:, first:last], (((0,), (0,)), ((), ())),
             preferred_element_type=F32,
         )
-        out_ref[...] = picked.astype(BF16).reshape(out_ref.shape)
+
+    out_ref[:, :, :width] = take(chosen[0], 0, width).astype(BF16).reshape(n, BASE, width)
+    extra = take(chosen[1], 0, half) + take(chosen[2], half, width)
+    out_ref[:, :, width:] = extra.astype(BF16).reshape(n, BASE, half)
 
     here = (lane == me).astype(F32)
     meta = jnp.zeros((1, n), F32)
@@ -146,10 +150,9 @@
     return pl.pallas_call(
         plan_kernel,
         in_specs=[pl.BlockSpec(memory_space=pltpu.SMEM), vmem, vmem],
-        out_specs=[vmem] * 4,
+        out_specs=[vmem] * 3,
         out_shape=[
-            jax.ShapeDtypeStruct((128, BASE, width), BF16),
-            jax.ShapeDtypeStruct((128, SPARE, width), BF16),
+            jax.ShapeDtypeStruct((128, BASE, width * CAP // BASE), BF16),
             jax.ShapeDtypeStruct(ids.shape, jnp.int32),
             jax.ShapeDtypeStruct((1, 128), jnp.int32),
         ],
@@ -166,13 +169,17 @@
 
 def spread_kernel(flags_ref, got_ref, *refs):
     outs, parts_ref, sems = refs[:-2], refs[-2], refs[-1]
-    n, spare, width = got_ref.shape
-    got = got_ref[...].reshape(n * spare, width)
-    row = lax.broadcasted_iota(jnp.int32, (n, n * spare), 0)
-    column = lax.broadcasted_iota(jnp.int32, (n, n * spare), 1)
+    n, lines, wide = got_ref.shape
+    width = parts_ref.shape[2]
+    half = width // 2
+    got = got_ref[:, :, width:].reshape(n * lines, half)
+    row = lax.broadcasted_iota(jnp.int32, (n, n * lines), 0)
+    column = lax.broadcasted_iota(jnp.int32, (n, n * lines), 1)
     for s in range(SPARE):
-        take = (row * spare + s == column).astype(BF16)
-        parts_ref[s] = jnp.dot(take, got, preferred_element_type=F32).astype(BF16)
+        for t in range(2):
+            take = (row * lines + 2 * s + t == column).astype(BF16)
+            part = jnp.dot(take, got, preferred_element_type=F32)
+            parts_ref[s, :, t * half : (t + 1) * half] = part.astype(BF16)
     copies = [
         pltpu.make_async_copy(parts_ref.at[i if i < SPARE else flags_ref[i - SPARE]], out, sems.at[i])
         for i, out in enumerate(outs)
@@ -184,7 +191,8 @@
 
 
 def spread(flags, got):
-    n, spare, width = got.shape
+    n, _, wide = got.shape
+    width = wide * BASE // CAP
     count = SPARE + len(DIRS)
     return pl.pallas_call(
         spread_kernel,
@@ -200,27 +208,47 @@
 PANEL = 512
 
 
-def fetch(weights, scratch):
-    gate, up, down = weights
+def fetcher(choices, scratch):
+    hid_ref, gate_ref, up_ref, down_ref, sems = scratch
+    blocks = gate_ref.shape[0]
+
+    def copies(weights, i):
+        gate, up, down = weights
+        if i < blocks:
+            at = pl.ds(i * BLOCK, BLOCK)
+            pltpu.make_async_copy(gate.at[0, :, at], gate_ref.at[i], sems.at[2 * i]).start()
+            pltpu.make_async_copy(up.at[0, :, at], up_ref.at[i], sems.at[2 * i + 1]).start()
+        else:
+            c = i - blocks
+            at = pl.ds(c * PANEL, PANEL)
+            pltpu.make_async_copy(down.at[0, :, at], down_ref.at[c], sems.at[2 * blocks + c]).start()
+
+    def start(i):
+        for condition, weights in choices:
+            if condition is None:
+                copies(weights, i)
+            else:
+                pl.when(condition)(functools.partial(copies, weights, i))
+
+    return start
+
+
+def ffn_rows(x_ref, out_ref, scratch, start):
     hid_ref, gate_ref, up_ref, down_ref, sems = scratch
     blocks, panels = gate_ref.shape[0], down_ref.shape[0]
-    for p in range(blocks):
-        at = pl.ds(p * BLOCK, BLOCK)
-        pltpu.make_async_copy(gate.at[0, :, at], gate_ref.at[p], sems.at[2 * p]).start()
-        pltpu.make_async_copy(up.at[0, :, at], up_ref.at[p], sems.at[2 * p + 1]).start()
-    for c in range(panels):
-        at = pl.ds(c * PANEL, PANEL)
-        pltpu.make_async_copy(down.at[0, :, at], down_ref.at[c], sems.at[2 * blocks + c]).start()
-
-
-def ffn_rows(x_ref, out_ref, scratch):
-    hid_ref, gate_ref, up_ref, down_ref, sems = scratch
-    blocks, panels = gate_ref.shape[0], down_ref.shape[0]
+    later = list(range(2, blocks + panels))
+    per = -(-len(later) // blocks)
 
     @pl.loop(0, blocks)
     def _(p):
         pltpu.make_async_copy(gate_ref.at[p], gate_ref.at[p], sems.at[2 * p]).wait()
         pltpu.make_async_copy(up_ref.at[p], up_ref.at[p], sems.at[2 * p + 1]).wait()
+        for q in range(blocks):
+            @pl.when(p == q)
+            def _():
+                for i in later[q * per : (q + 1) * per]:
+                    start(i)
+
         x = x_ref[...]
         gate_act = jnp.dot(x, gate_ref[p], preferred_element_type=F32)
         upper = jnp.dot(x, up_ref[p], preferred_element_type=F32)
@@ -255,14 +283,17 @@
 
 
 def ffn_kernel(x_ref, gate, up, down, out_ref, rows_ref, *scratch):
-    fetch((gate, up, down), scratch)
-    rows_ref[...] = x_ref[...].reshape(rows_ref.shape)
-    ffn_rows(rows_ref, out_ref, scratch)
+    start = fetcher([(None, (gate, up, down))], scratch)
+    start(0)
+    start(1)
+    rows, width = rows_ref.shape
+    rows_ref[...] = x_ref[:, :, :width].reshape(rows, width)
+    ffn_rows(rows_ref, out_ref, scratch, start)
 
 
 def ffn(x, gate_mat, up_mat, down_mat):
-    n, slots, width = x.shape
-    inner = gate_mat.shape[2]
+    n, slots, _ = x.shape
+    width, inner = gate_mat.shape[1:]
     rows = n * slots
     return pl.pallas_call(
         ffn_kernel,
@@ -294,17 +325,12 @@
         for copy in arriving:
             copy.start()
 
-        @pl.when(flags_ref[8] == 1)
-        def _():
-            fetch(own, scratch)
-
-        @pl.when(flags_ref[8] == 0)
-        def _():
-            fetch(other, scratch)
-
+        start = fetcher([(flags_ref[8] == 1, own), (flags_ref[8] == 0, other)], scratch)
+        start(0)
+        start(1)
         for copy in arriving:
             copy.wait()
-        ffn_rows(rows_ref, done_ref, scratch)
+        ffn_rows(rows_ref, done_ref, scratch, start)
         leaving = [
             pltpu.make_async_copy(done_ref.at[at], out, sems.at[base + g])
             for g, (out, at) in enumerate(zip(outs, parts))
@@ -429,29 +455,28 @@
     return lax.all_to_all(x, "expert", split_axis=0, concat_axis=0, tiled=True)
 
 
-def relayed(scores, w_gate, w_up, w_down, base, spare, slots, meta):
+def relayed(scores, w_gate, w_up, w_down, outgoing, slots, meta):
     n = lax.axis_size("expert")
     flags = meta[0]
     swap = [(i, i ^ 1) for i in range(n)]
     own = (w_gate, w_up, w_down)
     other = [lax.ppermute(w, "expert", swap) for w in own]
-    got_spare, base, *other = lax.optimization_barrier((exchange(spare), base, *other))
-    got_base = exchange(base)
-    parts = spread(flags, got_spare)
+    got, *other = lax.optimization_barrier((exchange(outgoing), *other))
+    parts = spread(flags, got)
     kept, sent = parts[:SPARE], parts[SPARE:]
     hopped = [
         lax.ppermute(x, "expert", hop_pairs(axis, step, n)) for x, (axis, step) in zip(sent, DIRS)
     ]
     first = hot_ffn(flags, kept, own, other)
-    first, early = lax.optimization_barrier((first, hopped[:3]))
+    got, first, hopped[0] = lax.optimization_barrier((got, first, hopped[0]))
+    served = ffn(got, *own)
+    served, early = lax.optimization_barrier((served, hopped[:3]))
     second = hot_ffn(flags, early, own, other)
     third = hot_ffn(flags, hopped[3:], own, other)
     back = [
         lax.ppermute(x, "expert", hop_pairs(axis, -step, n))
         for x, (axis, step) in zip(list(second) + list(third), DIRS)
     ]
-    got_base, *_ = lax.optimization_barrier((got_base, *third))
-    served = ffn(got_base, *own)
     return mix(scores, slots, exchange(join(flags, served, first, back)))
 
 
@@ -482,8 +507,8 @@
 
 def body(tokens, ids, scores, w_gate, w_up, w_down):
     me = lax.axis_index("expert").astype(jnp.int32).reshape(1)
-    base, spare, slots, meta = plan(me, ids, tokens)
-    mixed = relayed(scores, w_gate, w_up, w_down, base, spare, slots, meta)
+    outgoing, slots, meta = plan(me, ids, tokens)
+    mixed = relayed(scores, w_gate, w_up, w_down, outgoing, slots, meta)
     return lax.cond(
         meta[0, 10] == 1,
         lambda mixed, *rest: mixed,

time: 173 us -> 173 us (level)
  starting transfers between devices: 43.5 us -> 18.2 us
  blocking collectives: 29.1 us -> 51.7 us
  Pallas kernels: 22.6 us -> 43.1 us
  waiting for transfers between devices: 69.9 us -> 53.1 us
    ppermute x6, waiting for transfers between devices: 24.3 us -> 0.91 us  [relayed(): lax.ppermute(x, 'expert', hop_pairs(axis, step, n))]
    pallas_call x3, Pallas kernels: 2.35 us -> 25.6 us  [hot_ffn(): pl.pallas_call(functools.partial(hot_kernel, len(xs)), in_specs=[SMEM] +...]
    all_to_all x1, blocking collectives: 29.1 us -> 51.7 us  [exchange(): return lax.all_to_all(x, 'expert', split_axis=0, concat_axis=0, tiled=True)]
    ppermute x6, starting transfers between devices: 20.8 us -> 2.52 us  [relayed(): lax.ppermute(x, 'expert', hop_pairs(axis, -step, n))]
    ppermute x6, waiting for transfers between devices: 5.09 us -> 11.8 us  [relayed(): lax.ppermute(x, 'expert', hop_pairs(axis, -step, n))]
    ppermute x6, starting transfers between devices: 9.68 us -> 5.93 us  [relayed(): lax.ppermute(x, 'expert', hop_pairs(axis, step, n))]
    all_to_all x2 -> x1, starting transfers between devices: 11.2 us -> 7.81 us  [exchange(): return lax.all_to_all(x, 'expert', split_axis=0, concat_axis=0, tiled=True)]
    pallas_call x1, Pallas kernels: 3.58 us -> 1.69 us  [join(): pl.pallas_call(join_kernel, in_specs=[SMEM, VMEM] + [HBM] * (SPARE + len(...]
  transfers between devices with their start and end apart: 17 -> 16, of which waited for: 4 -> 6; matrix products, arithmetic and copies ran while one was open for 1% -> 1% of each run, Pallas kernels for 10% -> 21%
where the time goes in v1:
time: 173 us
  waiting for transfers between devices  53.1 us (31%)
  blocking collectives  51.7 us (30%)
  Pallas kernels  43.1 us (25%)
  starting transfers between devices  18.2 us (11%)
  local copies, waits for them, and re-layouts  6.02 us (3%)
    all_to_all x1, blocking collectives, exchange(): return lax.all_to_all(x, 'expert', split_axis=0, concat_axis=0, tiled=True)  51.7 us
    all_to_all x1, waiting for transfers between devices, exchange(): return lax.all_to_all(x, 'expert', split_axis=0, concat_axis=0, tiled=True)  40.4 us
    pallas_call x3, Pallas kernels, hot_ffn(): pl.pallas_call(functools.partial(hot_kernel, len(xs)), in_specs=[SMEM] +...  25.6 us
    ppermute x6, waiting for transfers between devices, relayed(): lax.ppermute(x, 'expert', hop_pairs(axis, -step, n))  11.8 us
    all_to_all x1, starting transfers between devices, exchange(): return lax.all_to_all(x, 'expert', split_axis=0, concat_axis=0, tiled=True)  7.81 us
    pallas_call x1, Pallas kernels, ffn(): pl.pallas_call(ffn_kernel, in_specs=[VMEM] + [HBM] * 3, out_specs=VMEM, o...  7.74 us
    ppermute x6, starting transfers between devices, relayed(): lax.ppermute(x, 'expert', hop_pairs(axis, step, n))  5.93 us
    unnamed x26, local copies, waits for them, and re-layouts  5.44 us
  transfers between devices with their start and end apart: 16, of which 6 were waited for; matrix products, arithmetic and copies ran while one was open for 1% of the time, Pallas kernels for 21%

profile of v1, /device:TPU:1, one launch (start us, length us, event | category | flops | bytes accessed | tf_op | source)
XLA Modules:
  0.0 173.0 jit_solution(3259976133031596979)
XLA Ops:
  0.0 1.4 collective-permute-start
  1.9 0.8 copy.14.ids_ref
  2.7 3.4 %plan.1 = (bf16[128,4,3072]{2,1,0:T(4,128)(2,1)S(1)}, s32[64,8]{1,0:T(8,128)S(1)}, s32[1,128]{1,0:T(1,128)S(1)}) custom-call(s32[1]{0:T(128)} %bitcast.10.me_ref, s32[64,8]{1,0:T(8,128)S(1)} %copy.14.ids_ref, bf16[64,2048]{1,0:T(8,128)(2,1)} %tok_ref.1), custom_call_target="tpu_custom_call" | custom-call | tf_op jit(solution)/shard_map/plan/pallas_call | solution.py:150
  6.1 51.7 %all_to_all.19.got_ref.x_ref = bf16[128,4,3072]{2,1,0:T(4,128)(2,1)S(1)} all-to-all(bf16[128,4,3072]{2,1,0:T(4,128)(2,1)S(1)} %get-tuple-element.60), channel_id=1, replica_groups=mesh['expert'=128] {'expert'}, dimensions={0} | all-to-all | bytes 6291456 | tf_op jit(solution)/shard_map/all_to_all | solution.py:455
  57.8 2.9 %spread.1 = (bf16[128,2048]{1,0:T(8,128)(2,1)S(1)}, bf16[128,2048]{1,0:T(8,128)(2,1)S(1)}, bf16[128,2048]{1,0:T(8,128)(2,1)}, bf16[128,2048]{1,0:T(8,128)(2,1)},...) custom-call(s32[128]{0:T(128)S(1)} %bitcast.36, ...), custom_call_target="tpu_custom_call" | custom-call | tf_op jit(solution)/shard_map/spread/pallas_call | solution.py:197
  60.7 0.8 copy-done.5
  61.5 0.8 copy-done.6
  62.5 2.4 %collective-permute-start.4 = (bf16[128,2048]{1,0:T(8,128)(2,1)}, bf16[128,2048]{1,0:T(8,128)(2,1)}, u32[]{:S(2)}, u32[]{:S(2)}) collective-permute-start(bf16[128,2048]{1,0:T(8,128)(2,1)} %get-tuple-element.72), channel_id=1, source_target_pairs={{0,96},{1,97},{2,98},{3,99},{4,100},{5,101},{6,102},{7,103},{8,104... | collective-permute-start | bytes 1572872 | tf_op jit(solution)/shard_map/ppermute | solution.py:468
  65.0 2.6 %collective-permute-start.11 = (bf16[128,2048]{1,0:T(8,128)(2,1)}, bf16[128,2048]{1,0:T(8,128)(2,1)}, u32[]{:S(2)}, u32[]{:S(2)}) collective-permute-start(bf16[128,2048]{1,0:T(8,128)(2,1)} %get-tuple-element.85), channel_id=1, source_target_pairs={{0,6},{1,7},{2,0},{3,1},{4,2},{5,3},{6,4},{7,5},{8,14},{9,15},{10,... | collective-permute-start | bytes 1572872 | tf_op jit(solution)/shard_map/ppermute | solution.py:468
  67.6 7.6 %hot_ffn.3 = (bf16[128,2048]{1,0:T(8,128)(2,1)}, bf16[128,2048]{1,0:T(8,128)(2,1)}) custom-call(s32[128]{0:T(128)} %bitcast.37, bf16[128,2048]{1,0:T(8,128)(2,1)} %copy-done.5, bf16[128,2048]{1,0:T(8,128)(2,1)} %copy-done.6, bf16[1,2048,768]{2,1,0:T(8,128)(2,1)} %refs_3_.5, bf16[1,2048,768]{2,1,0:T(8,128)(2,1)} %refs_4_.5, bf16[1,768,2048]{2,1,0:T(8,128)(2,1)} %refs_5_.3, ...), custom_call_target="tpu_custom_call" | custom-call | flops 2415919104 | bytes 9437184 | tf_op jit(solution)/shard_map/hot_ffn/pallas_call | solution.py:348
  75.2 0.9 collective-permute-done.3.refs_0_
  76.7 7.7 %ffn.1.served_ref = bf16[512,2048]{1,0:T(8,128)(2,1)S(1)} custom-call(bf16[128,4,3072]{2,1,0:T(4,128)(2,1)S(1)} %all_to_all.19.got_ref.x_ref, bf16[1,2048,768]{2,1,0:T(8,128)(2,1)} %refs_3_.5, bf16[1,2048,768]{2,1,0:T(8,128)(2,1)} %refs_4_.5, bf16[1,768,2048]{2,1,0:T(8,128)(2,1)} %refs_5_.3), custom_call_target="tpu_custom_call" | custom-call | flops 4831838208 | bytes 9437184 | tf_op jit(solution)/shard_map/ffn/pallas_call | solution.py:298
  84.5 1.3 copy-done.1
  85.8 8.8 %hot_ffn.4 = (bf16[128,2048]{1,0:T(8,128)(2,1)}, bf16[128,2048]{1,0:T(8,128)(2,1)}, bf16[128,2048]{1,0:T(8,128)(2,1)}) custom-call(s32[128]{0:T(128)} %bitcast.38, bf16[128,2048]{1,0:T(8,128)(2,1)} %collective-permute-done.3.refs_0_, bf16[128,2048]{1,0:T(8,128)(2,1)} %collective-permute-done.4.refs_1_, bf16[128,2048]{1,0:T(8,128)(2,1)} %collective-permute-done.5.refs_2_, ...), custom_call_target="tpu_custom_call" | custom-call | flops 3623878656 | bytes 9437184 | tf_op jit(solution)/shard_map/hot_ffn/pallas_call | solution.py:348
  94.7 1.5 collective-permute-start.7
  96.3 9.2 %hot_ffn.5 = (bf16[128,2048]{1,0:T(8,128)(2,1)}, bf16[128,2048]{1,0:T(8,128)(2,1)}, bf16[128,2048]{1,0:T(8,128)(2,1)}) custom-call(s32[128]{0:T(128)} %bitcast.39, bf16[128,2048]{1,0:T(8,128)(2,1)} %collective-permute-done.9.refs_0_, bf16[128,2048]{1,0:T(8,128)(2,1)} %collective-permute-done.10.refs_1_, bf16[128,2048]{1,0:T(8,128)(2,1)} %collective-permute-done.11.refs_2_, ...), custom_call_target="tpu_custom_call" | custom-call | flops 3623878656 | bytes 9437184 | tf_op jit(solution)/shard_map/hot_ffn/pallas_call | solution.py:348
  105.6 0.7 collective-permute-done.6.refs_2_
  106.3 0.8 collective-permute-start.14
  107.6 10.1 %collective-permute-done.12.refs_5_ = bf16[128,2048]{1,0:T(8,128)(2,1)S(1)} collective-permute-done((bf16[128,2048]{1,0:T(8,128)(2,1)}, bf16[128,2048]{1,0:T(8,128)(2,1)S(1)}, u32[]{:S(2)}, u32[]{:S(2)}) %collective-permute-start.12) | collective-permute-done | bytes 524320 | tf_op jit(solution)/shard_map/ppermute | solution.py:477
  118.3 1.7 join.1
  120.0 1.6 copy-done
  121.6 7.8 %all-to-all-start.3 = ((bf16[128,4,3072]{2,1,0:T(4,128)(2,1)}), bf16[128,4,3072]{2,1,0:T(4,128)(2,1)S(1)}, u32[]{:S(2)}, u32[]{:S(2)}) async-start(bf16[128,4,3072]{2,1,0:T(4,128)(2,1)} %copy-done), calls=%async_computation.3 | async-start | bytes 6291456 | tf_op jit(solution)/shard_map/all_to_all | solution.py:455
  130.8 40.4 %all-to-all-done.3.ans_ref = bf16[128,4,3072]{2,1,0:T(4,128)(2,1)S(1)} async-done(((bf16[128,4,3072]{2,1,0:T(4,128)(2,1)}), bf16[128,4,3072]{2,1,0:T(4,128)(2,1)S(1)}, u32[]{:S(2)}, u32[]{:S(2)}) %all-to-all-start.3) | async-done | bytes 3145760 | tf_op jit(solution)/shard_map/all_to_all | solution.py:455
  171.1 1.9 %mix.1 = bf16[64,2048]{1,0:T(8,128)(2,1)} custom-call(f32[64,8]{1,0:T(8,128)S(1)} %copy.15.score_ref, s32[64,8]{1,0:T(8,128)S(1)} %get-tuple-element.59.slot_ref, bf16[128,4,3072]{2,1,0:T(4,128)(2,1)S(1)} %all-to-all-done.3.ans_ref), custom_call_target="tpu_custom_call" | custom-call | tf_op jit(solution)/shard_map/mix/pallas_call | solution.py:444
  (45 shorter events, 3.4 us)
Async XLA Ops:
  0.0 57.8 %collective-permute-start = (bf16[1,2048,768]{2,1,0:T(8,128)(2,1)}, bf16[1,2048,768]{2,1,0:T(8,128)(2,1)}, u32[]{:S(2)}, u32[]{:S(2)}) collective-permute-start(bf16[1,2048,768]{2,1,0:T(8,128)(2,1)} %refs_3_.5), channel_id=1, source_target_pairs={{0,1},{1,0},{2,3},{3,2},{4,5},{5,4},{6,7},{7,6},{8,9},{9,8},{10,11... | collective-permute-start | bytes 9437192 | tf_op jit(solution)/shard_map/ppermute | solution.py:463
  1.4 56.3 %collective-permute-start.1 = (bf16[1,2048,768]{2,1,0:T(8,128)(2,1)}, bf16[1,2048,768]{2,1,0:T(8,128)(2,1)}, u32[]{:S(2)}, u32[]{:S(2)}) collective-permute-start(bf16[1,2048,768]{2,1,0:T(8,128)(2,1)} %refs_4_.5), channel_id=1, source_target_pairs={{0,1},{1,0},{2,3},{3,2},{4,5},{5,4},{6,7},{7,6},{8,9},{9,8},{10,11... | collective-permute-start | bytes 9437192 | tf_op jit(solution)/shard_map/ppermute | solution.py:463
  1.4 56.3 %collective-permute-start.2 = (bf16[1,768,2048]{2,1,0:T(8,128)(2,1)}, bf16[1,768,2048]{2,1,0:T(8,128)(2,1)}, u32[]{:S(2)}, u32[]{:S(2)}) collective-permute-start(bf16[1,768,2048]{2,1,0:T(8,128)(2,1)} %refs_5_.3), channel_id=1, source_target_pairs={{0,1},{1,0},{2,3},{3,2},{4,5},{5,4},{6,7},{7,6},{8,9},{9,8},{10,11... | collective-permute-start | bytes 9437192 | tf_op jit(solution)/shard_map/ppermute | solution.py:463
  6.1 54.6 %copy-start.7 = (s32[1,128]{1,0:T(1,128)}, s32[1,128]{1,0:T(1,128)S(1)}, u32[]{:S(2)}) copy-start(s32[1,128]{1,0:T(1,128)S(1)} %get-tuple-element.58) | copy-start | bytes 1540
  62.3 13.8 %collective-permute-start.3 = (bf16[128,2048]{1,0:T(8,128)(2,1)}, bf16[128,2048]{1,0:T(8,128)(2,1)}, u32[]{:S(2)}, u32[]{:S(2)}) collective-permute-start(bf16[128,2048]{1,0:T(8,128)(2,1)} %get-tuple-element.69), channel_id=1, source_target_pairs={{0,32},{1,33},{2,34},{3,35},{4,36},{5,37},{6,38},{7,39},{8,40},{9,... | collective-permute-start | bytes 1572872 | tf_op jit(solution)/shard_map/ppermute | solution.py:468
  62.5 23.2 %collective-permute-start.4 = (bf16[128,2048]{1,0:T(8,128)(2,1)}, bf16[128,2048]{1,0:T(8,128)(2,1)}, u32[]{:S(2)}, u32[]{:S(2)}) collective-permute-start(bf16[128,2048]{1,0:T(8,128)(2,1)} %get-tuple-element.72), channel_id=1, source_target_pairs={{0,96},{1,97},{2,98},{3,99},{4,100},{5,101},{6,102},{7,103},{8,104... | collective-permute-start | bytes 1572872 | tf_op jit(solution)/shard_map/ppermute | solution.py:468
  65.0 20.8 %collective-permute-start.5 = (bf16[128,2048]{1,0:T(8,128)(2,1)S(1)}, bf16[128,2048]{1,0:T(8,128)(2,1)}, u32[]{:S(2)}, u32[]{:S(2)}) collective-permute-start(bf16[128,2048]{1,0:T(8,128)(2,1)S(1)} %get-tuple-element.73), channel_id=1, source_target_pairs={{0,8},{1,9},{2,10},{3,11},{4,12},{5,13},{6,14},{7,15},{8,16},{9,17... | collective-permute-start | bytes 1572872 | tf_op jit(solution)/shard_map/ppermute | solution.py:468
  65.0 31.2 %collective-permute-start.10 = (bf16[128,2048]{1,0:T(8,128)(2,1)}, bf16[128,2048]{1,0:T(8,128)(2,1)}, u32[]{:S(2)}, u32[]{:S(2)}) collective-permute-start(bf16[128,2048]{1,0:T(8,128)(2,1)} %get-tuple-element.84), channel_id=1, source_target_pairs={{0,2},{1,3},{2,4},{3,5},{4,6},{5,7},{6,0},{7,1},{8,10},{9,11},{10,... | collective-permute-start | bytes 1572872 | tf_op jit(solution)/shard_map/ppermute | solution.py:468
  65.0 31.2 %collective-permute-start.11 = (bf16[128,2048]{1,0:T(8,128)(2,1)}, bf16[128,2048]{1,0:T(8,128)(2,1)}, u32[]{:S(2)}, u32[]{:S(2)}) collective-permute-start(bf16[128,2048]{1,0:T(8,128)(2,1)} %get-tuple-element.85), channel_id=1, source_target_pairs={{0,6},{1,7},{2,0},{3,1},{4,2},{5,3},{6,4},{7,5},{8,14},{9,15},{10,... | collective-permute-start | bytes 1572872 | tf_op jit(solution)/shard_map/ppermute | solution.py:468
  76.1 20.1 %collective-permute-start.9 = (bf16[128,2048]{1,0:T(8,128)(2,1)}, bf16[128,2048]{1,0:T(8,128)(2,1)}, u32[]{:S(2)}, u32[]{:S(2)}) collective-permute-start(bf16[128,2048]{1,0:T(8,128)(2,1)} %get-tuple-element.83), channel_id=1, source_target_pairs={{0,24},{1,25},{2,26},{3,27},{4,28},{5,29},{6,30},{7,31},{8,0},{9,1... | collective-permute-start | bytes 1572872 | tf_op jit(solution)/shard_map/ppermute | solution.py:468
  94.6 11.7 %collective-permute-start.6 = (bf16[128,2048]{1,0:T(8,128)(2,1)}, bf16[128,2048]{1,0:T(8,128)(2,1)S(1)}, u32[]{:S(2)}, u32[]{:S(2)}) collective-permute-start(bf16[128,2048]{1,0:T(8,128)(2,1)} %get-tuple-element.80), channel_id=1, source_target_pairs={{0,96},{1,97},{2,98},{3,99},{4,100},{5,101},{6,102},{7,103},{8,104... | collective-permute-start | bytes 1572872 | tf_op jit(solution)/shard_map/ppermute | solution.py:477
  94.7 12.9 %collective-permute-start.7 = (bf16[128,2048]{1,0:T(8,128)(2,1)}, bf16[128,2048]{1,0:T(8,128)(2,1)}, u32[]{:S(2)}, u32[]{:S(2)}) collective-permute-start(bf16[128,2048]{1,0:T(8,128)(2,1)} %get-tuple-element.81), channel_id=1, source_target_pairs={{0,32},{1,33},{2,34},{3,35},{4,36},{5,37},{6,38},{7,39},{8,40},{9,... | collective-permute-start | bytes 1572872 | tf_op jit(solution)/shard_map/ppermute | solution.py:477
  96.1 22.1 %copy-start.2 = (bf16[512,2048]{1,0:T(8,128)(2,1)S(1)}, bf16[512,2048]{1,0:T(8,128)(2,1)}, u32[]{:S(2)}) copy-start(bf16[512,2048]{1,0:T(8,128)(2,1)} %copy-done.1) | copy-start | bytes 6291460
  96.1 22.1 %copy-start.3 = (bf16[128,2048]{1,0:T(8,128)(2,1)S(1)}, bf16[128,2048]{1,0:T(8,128)(2,1)}, u32[]{:S(2)}) copy-start(bf16[128,2048]{1,0:T(8,128)(2,1)} %get-tuple-element.75.refs_0_) | copy-start | bytes 1572868
  96.1 22.1 %copy-start.4 = (bf16[128,2048]{1,0:T(8,128)(2,1)S(1)}, bf16[128,2048]{1,0:T(8,128)(2,1)}, u32[]{:S(2)}) copy-start(bf16[128,2048]{1,0:T(8,128)(2,1)} %get-tuple-element.76.refs_1_) | copy-start | bytes 1572868
  96.2 22.1 %copy-start.8 = (s32[1,128]{1,0:T(1,128)S(1)}, s32[1,128]{1,0:T(1,128)}, u32[]{:S(2)}) copy-start(s32[1,128]{1,0:T(1,128)} %copy-done.7) | copy-start | bytes 1540
  96.2 11.4 %collective-permute-start.8 = (bf16[128,2048]{1,0:T(8,128)(2,1)}, bf16[128,2048]{1,0:T(8,128)(2,1)}, u32[]{:S(2)}, u32[]{:S(2)}) collective-permute-start(bf16[128,2048]{1,0:T(8,128)(2,1)} %get-tuple-element.82), channel_id=1, source_target_pairs={{0,24},{1,25},{2,26},{3,27},{4,28},{5,29},{6,30},{7,31},{8,0},{9,1... | collective-permute-start | bytes 1572872 | tf_op jit(solution)/shard_map/ppermute | solution.py:477
  105.5 12.3 %collective-permute-start.12 = (bf16[128,2048]{1,0:T(8,128)(2,1)}, bf16[128,2048]{1,0:T(8,128)(2,1)S(1)}, u32[]{:S(2)}, u32[]{:S(2)}) collective-permute-start(bf16[128,2048]{1,0:T(8,128)(2,1)} %get-tuple-element.86), channel_id=1, source_target_pairs={{0,8},{1,9},{2,10},{3,11},{4,12},{5,13},{6,14},{7,15},{8,16},{9,17... | collective-permute-start | bytes 1572872 | tf_op jit(solution)/shard_map/ppermute | solution.py:477
  105.5 12.2 %collective-permute-start.13 = (bf16[128,2048]{1,0:T(8,128)(2,1)}, bf16[128,2048]{1,0:T(8,128)(2,1)S(1)}, u32[]{:S(2)}, u32[]{:S(2)}) collective-permute-start(bf16[128,2048]{1,0:T(8,128)(2,1)} %get-tuple-element.87), channel_id=1, source_target_pairs={{0,6},{1,7},{2,0},{3,1},{4,2},{5,3},{6,4},{7,5},{8,14},{9,15},{10,... | collective-permute-start | bytes 1572872 | tf_op jit(solution)/shard_map/ppermute | solution.py:477
  106.3 11.9 %collective-permute-start.14 = (bf16[128,2048]{1,0:T(8,128)(2,1)}, bf16[128,2048]{1,0:T(8,128)(2,1)S(1)}, u32[]{:S(2)}, u32[]{:S(2)}) collective-permute-start(bf16[128,2048]{1,0:T(8,128)(2,1)} %get-tuple-element.88), channel_id=1, source_target_pairs={{0,2},{1,3},{2,4},{3,5},{4,6},{5,7},{6,0},{7,1},{8,10},{9,11},{10,... | collective-permute-start | bytes 1572872 | tf_op jit(solution)/shard_map/ppermute | solution.py:477
  121.6 8.4 %copy-start.11 = (f32[64,8]{0,1:T(8,128)S(1)}, f32[64,8]{0,1:T(8,128)}, u32[]{:S(2)}) copy-start(f32[64,8]{0,1:T(8,128)} %param.10) | copy-start | bytes 6148
  121.6 51.4 %copy-start.10 = (bf16[64,2048]{1,0:T(8,128)(2,1)S(1)}, bf16[64,2048]{1,0:T(8,128)(2,1)}, u32[]{:S(2)}) copy-start(bf16[64,2048]{1,0:T(8,128)(2,1)} %tok_ref.1) | copy-start | bytes 786436
  121.6 51.4 %copy-start.12 = (s32[64,8]{0,1:T(8,128)S(1)}, s32[64,8]{0,1:T(8,128)}, u32[]{:S(2)}) copy-start(s32[64,8]{0,1:T(8,128)} %param.9) | copy-start | bytes 6148
  121.6 49.5 %all-to-all-start.3 = ((bf16[128,4,3072]{2,1,0:T(4,128)(2,1)}), bf16[128,4,3072]{2,1,0:T(4,128)(2,1)S(1)}, u32[]{:S(2)}, u32[]{:S(2)}) async-start(bf16[128,4,3072]{2,1,0:T(4,128)(2,1)} %copy-done), calls=%async_computation.3 | async-start | bytes 6291456 | tf_op jit(solution)/shard_map/all_to_all | solution.py:455
  (4 other events, 4.6 us)

commit v2 on v1

--- a/solution.py
+++ b/solution.py
@@ -467,17 +467,15 @@
     hopped = [
         lax.ppermute(x, "expert", hop_pairs(axis, step, n)) for x, (axis, step) in zip(sent, DIRS)
     ]
-    first = hot_ffn(flags, kept, own, other)
-    got, first, hopped[0] = lax.optimization_barrier((got, first, hopped[0]))
     served = ffn(got, *own)
-    served, early = lax.optimization_barrier((served, hopped[:3]))
-    second = hot_ffn(flags, early, own, other)
-    third = hot_ffn(flags, hopped[3:], own, other)
+    served, kept, early = lax.optimization_barrier((served, kept, hopped[:2]))
+    first = hot_ffn(flags, list(kept) + early, own, other)
+    second = hot_ffn(flags, hopped[2:], own, other)
     back = [
         lax.ppermute(x, "expert", hop_pairs(axis, -step, n))
-        for x, (axis, step) in zip(list(second) + list(third), DIRS)
+        for x, (axis, step) in zip(list(first[SPARE:]) + list(second), DIRS)
     ]
-    return mix(scores, slots, exchange(join(flags, served, first, back)))
+    return mix(scores, slots, exchange(join(flags, served, first[:SPARE], back)))
 
 
 def expert_ffn(rows, gate_mat, up_mat, down_mat):

time: 173 us -> 180 us (1.040)
  Pallas kernels: 43.1 us -> 18.9 us
  starting transfers between devices: 18.2 us -> 38.7 us
  waiting for transfers between devices: 53.1 us -> 59.6 us
  local copies, waits for them, and re-layouts: 6.02 us -> 9.66 us
    pallas_call x3 -> x2, Pallas kernels: 25.6 us -> 1.91 us  [hot_ffn(): pl.pallas_call(functools.partial(hot_kernel, len(xs)), in_specs=[SMEM] +...]
    all_to_all x1, starting transfers between devices: 7.81 us -> 18.6 us  [exchange(): return lax.all_to_all(x, 'expert', split_axis=0, concat_axis=0, tiled=True)]
    ppermute x6, starting transfers between devices: 2.52 us -> 12.6 us  [relayed(): lax.ppermute(x, 'expert', hop_pairs(axis, -step, n))]
    ppermute x6, waiting for transfers between devices: 0.91 us -> 8.69 us  [relayed(): lax.ppermute(x, 'expert', hop_pairs(axis, step, n))]
    unnamed x26 -> x32, local copies, waits for them, and re-layouts: 5.44 us -> 9.07 us
  transfers between devices with their start and end apart: 16 -> 16, of which waited for: 6 -> 7; matrix products, arithmetic and copies ran while one was open for 1% -> 1% of each run, Pallas kernels for 21% -> 7%
where the time goes in v2:
time: 180 us; the launch traced here: 179 us
  waiting for transfers between devices  59.6 us (33%)
  blocking collectives  51.7 us (29%)
  starting transfers between devices  38.7 us (22%)
  Pallas kernels  18.9 us (10%)
  local copies, waits for them, and re-layouts  9.66 us (5%)
    all_to_all x1, blocking collectives, exchange(): return lax.all_to_all(x, 'expert', split_axis=0, concat_axis=0, tiled=True)  51.7 us
    all_to_all x1, waiting for transfers between devices, exchange(): return lax.all_to_all(x, 'expert', split_axis=0, concat_axis=0, tiled=True)  40.4 us
    all_to_all x1, starting transfers between devices, exchange(): return lax.all_to_all(x, 'expert', split_axis=0, concat_axis=0, tiled=True)  18.6 us
    ppermute x6, starting transfers between devices, relayed(): lax.ppermute(x, 'expert', hop_pairs(axis, -step, n))  12.6 us
    ppermute x6, waiting for transfers between devices, relayed(): lax.ppermute(x, 'expert', hop_pairs(axis, -step, n))  10.6 us
    unnamed x32, local copies, waits for them, and re-layouts  9.07 us
    ppermute x6, waiting for transfers between devices, relayed(): lax.ppermute(x, 'expert', hop_pairs(axis, step, n))  8.69 us
    pallas_call x1, Pallas kernels, ffn(): pl.pallas_call(ffn_kernel, in_specs=[VMEM] + [HBM] * 3, out_specs=VMEM, o...  7.74 us
  transfers between devices with their start and end apart: 16, of which 7 were waited for; matrix products, arithmetic and copies ran while one was open for 1% of the time, Pallas kernels for 7%

profile of v2, /device:TPU:1, one launch (start us, length us, event | category | flops | bytes accessed | tf_op | source)
XLA Modules:
  0.0 179.3 jit_solution(15223872467320375877)
XLA Ops:
  0.0 1.4 collective-permute-start
  2.7 3.4 %plan.1 = (bf16[128,4,3072]{2,1,0:T(4,128)(2,1)S(1)}, s32[64,8]{1,0:T(8,128)S(1)}, s32[1,128]{1,0:T(1,128)S(1)}) custom-call(s32[1]{0:T(128)} %bitcast.10.me_ref, s32[64,8]{1,0:T(8,128)S(1)} %copy.14.ids_ref, bf16[64,2048]{1,0:T(8,128)(2,1)} %tok_ref.1), custom_call_target="tpu_custom_call" | custom-call | tf_op jit(solution)/shard_map/plan/pallas_call | solution.py:150
  6.1 51.7 %all_to_all.19.x_ref.got_ref = bf16[128,4,3072]{2,1,0:T(4,128)(2,1)S(1)} all-to-all(bf16[128,4,3072]{2,1,0:T(4,128)(2,1)S(1)} %get-tuple-element.57), channel_id=1, replica_groups=mesh['expert'=128] {'expert'}, dimensions={0} | all-to-all | bytes 6291456 | tf_op jit(solution)/shard_map/all_to_all | solution.py:455
  57.8 2.4 %spread.1 = (bf16[128,2048]{1,0:T(8,128)(2,1)S(1)}, bf16[128,2048]{1,0:T(8,128)(2,1)S(1)}, bf16[128,2048]{1,0:T(8,128)(2,1)}, bf16[128,2048]{1,0:T(8,128)(2,1)},...) custom-call(s32[128]{0:T(128)S(1)} %bitcast.36, ...), custom_call_target="tpu_custom_call" | custom-call | tf_op jit(solution)/shard_map/spread/pallas_call | solution.py:197
  61.0 0.8 copy-done.4
  62.3 2.4 %collective-permute-start.8 = (bf16[128,2048]{1,0:T(8,128)(2,1)S(1)}, bf16[128,2048]{1,0:T(8,128)(2,1)S(1)}, u32[]{:S(2)}, u32[]{:S(2)}) collective-permute-start(bf16[128,2048]{1,0:T(8,128)(2,1)S(1)} %get-tuple-element.76), channel_id=1, source_target_pairs={{0,24},{1,25},{2,26},{3,27},{4,28},{5,29},{6,30},{7,31},{8,0},{9,1... | collective-permute-start | bytes 1572872 | tf_op jit(solution)/shard_map/ppermute | solution.py:468
  64.7 1.2 collective-permute-start.9
  66.2 8.0 %collective-permute-done.10.refs_3_ = bf16[128,2048]{1,0:T(8,128)(2,1)S(1)} collective-permute-done((bf16[128,2048]{1,0:T(8,128)(2,1)S(1)}, bf16[128,2048]{1,0:T(8,128)(2,1)S(1)}, u32[]{:S(2)}, u32[]{:S(2)}) %collective-permute-start.10) | collective-permute-done | bytes 524320 | tf_op jit(solution)/shard_map/ppermute | solution.py:468
  74.2 1.2 collective-permute-start.4
  78.4 1.1 collective-permute-start.11
  79.6 7.7 %ffn.1.served_ref = bf16[512,2048]{1,0:T(8,128)(2,1)S(1)} custom-call(bf16[128,4,3072]{2,1,0:T(4,128)(2,1)S(1)} %all_to_all.19.x_ref.got_ref, bf16[1,2048,768]{2,1,0:T(8,128)(2,1)} %refs_4_.3, bf16[1,2048,768]{2,1,0:T(8,128)(2,1)} %refs_5_.3, bf16[1,768,2048]{2,1,0:T(8,128)(2,1)} %refs_6_.3), custom_call_target="tpu_custom_call" | custom-call | flops 4831838208 | bytes 9437184 | tf_op jit(solution)/shard_map/ffn/pallas_call | solution.py:298
  87.4 1.3 copy-done.1
  89.0 9.5 %collective-permute-start.13 = (bf16[128,2048]{1,0:T(8,128)(2,1)}, bf16[128,2048]{1,0:T(8,128)(2,1)S(1)}, u32[]{:S(2)}, u32[]{:S(2)}) collective-permute-start(bf16[128,2048]{1,0:T(8,128)(2,1)} %get-tuple-element.81), channel_id=1, source_target_pairs={{0,6},{1,7},{2,0},{3,1},{4,2},{5,3},{6,4},{7,5},{8,14},{9,15},{10,... | collective-permute-start | bytes 1572872 | tf_op jit(solution)/shard_map/ppermute | solution.py:475
  98.6 1.1 hot_ffn.2
  99.8 1.4 collective-permute-start.6
  101.3 7.5 %collective-permute-done.12.refs_5_ = bf16[128,2048]{1,0:T(8,128)(2,1)S(1)} collective-permute-done((bf16[128,2048]{1,0:T(8,128)(2,1)}, bf16[128,2048]{1,0:T(8,128)(2,1)S(1)}, u32[]{:S(2)}, u32[]{:S(2)}) %collective-permute-start.12) | collective-permute-done | bytes 524320 | tf_op jit(solution)/shard_map/ppermute | solution.py:475
  108.7 2.4 %collective-permute-done.14.refs_7_ = bf16[128,2048]{1,0:T(8,128)(2,1)} collective-permute-done((bf16[128,2048]{1,0:T(8,128)(2,1)}, bf16[128,2048]{1,0:T(8,128)(2,1)}, u32[]{:S(2)}, u32[]{:S(2)}) %collective-permute-start.14) | collective-permute-done | bytes 524320 | tf_op jit(solution)/shard_map/ppermute | solution.py:475
  111.8 1.0 copy-done.5
  112.9 1.0 copy-done.6
  113.9 1.7 join.1
  115.6 1.6 copy-done
  117.2 18.6 %all-to-all-start.3 = ((bf16[128,4,3072]{2,1,0:T(4,128)(2,1)}), bf16[128,4,3072]{2,1,0:T(4,128)(2,1)S(1)}, u32[]{:S(2)}, u32[]{:S(2)}) async-start(bf16[128,4,3072]{2,1,0:T(4,128)(2,1)} %copy-done), calls=%async_computation.3 | async-start | bytes 6291456 | tf_op jit(solution)/shard_map/all_to_all | solution.py:455
  137.1 40.4 %all-to-all-done.3.ans_ref = bf16[128,4,3072]{2,1,0:T(4,128)(2,1)S(1)} async-done(((bf16[128,4,3072]{2,1,0:T(4,128)(2,1)}), bf16[128,4,3072]{2,1,0:T(4,128)(2,1)S(1)}, u32[]{:S(2)}, u32[]{:S(2)}) %all-to-all-start.3) | async-done | bytes 3145760 | tf_op jit(solution)/shard_map/all_to_all | solution.py:455
  177.5 1.8 %mix.1 = bf16[64,2048]{1,0:T(8,128)(2,1)} custom-call(f32[64,8]{1,0:T(8,128)S(1)} %copy.15.score_ref, s32[64,8]{1,0:T(8,128)S(1)} %get-tuple-element.56.slot_ref, bf16[128,4,3072]{2,1,0:T(4,128)(2,1)S(1)} %all-to-all-done.3.ans_ref), custom_call_target="tpu_custom_call" | custom-call | tf_op jit(solution)/shard_map/mix/pallas_call | solution.py:444
  (50 shorter events, 7.8 us)
Async XLA Ops:
  0.0 57.8 %collective-permute-start = (bf16[1,2048,768]{2,1,0:T(8,128)(2,1)}, bf16[1,2048,768]{2,1,0:T(8,128)(2,1)}, u32[]{:S(2)}, u32[]{:S(2)}) collective-permute-start(bf16[1,2048,768]{2,1,0:T(8,128)(2,1)} %refs_4_.3), channel_id=1, source_target_pairs={{0,1},{1,0},{2,3},{3,2},{4,5},{5,4},{6,7},{7,6},{8,9},{9,8},{10,11... | collective-permute-start | bytes 9437192 | tf_op jit(solution)/shard_map/ppermute | solution.py:463
  1.4 56.3 %collective-permute-start.1 = (bf16[1,2048,768]{2,1,0:T(8,128)(2,1)}, bf16[1,2048,768]{2,1,0:T(8,128)(2,1)}, u32[]{:S(2)}, u32[]{:S(2)}) collective-permute-start(bf16[1,2048,768]{2,1,0:T(8,128)(2,1)} %refs_5_.3), channel_id=1, source_target_pairs={{0,1},{1,0},{2,3},{3,2},{4,5},{5,4},{6,7},{7,6},{8,9},{9,8},{10,11... | collective-permute-start | bytes 9437192 | tf_op jit(solution)/shard_map/ppermute | solution.py:463
  1.4 56.3 %collective-permute-start.2 = (bf16[1,768,2048]{2,1,0:T(8,128)(2,1)}, bf16[1,768,2048]{2,1,0:T(8,128)(2,1)}, u32[]{:S(2)}, u32[]{:S(2)}) collective-permute-start(bf16[1,768,2048]{2,1,0:T(8,128)(2,1)} %refs_6_.3), channel_id=1, source_target_pairs={{0,1},{1,0},{2,3},{3,2},{4,5},{5,4},{6,7},{7,6},{8,9},{9,8},{10,11... | collective-permute-start | bytes 9437192 | tf_op jit(solution)/shard_map/ppermute | solution.py:463
  6.1 54.1 %copy-start.7 = (s32[1,128]{1,0:T(1,128)}, s32[1,128]{1,0:T(1,128)S(1)}, u32[]{:S(2)}) copy-start(s32[1,128]{1,0:T(1,128)S(1)} %get-tuple-element.55) | copy-start | bytes 1540
  61.8 12.4 %collective-permute-start.10 = (bf16[128,2048]{1,0:T(8,128)(2,1)S(1)}, bf16[128,2048]{1,0:T(8,128)(2,1)S(1)}, u32[]{:S(2)}, u32[]{:S(2)}) collective-permute-start(bf16[128,2048]{1,0:T(8,128)(2,1)S(1)} %get-tuple-element.78), channel_id=1, source_target_pairs={{0,6},{1,7},{2,0},{3,1},{4,2},{5,3},{6,4},{7,5},{8,14},{9,15},{10,... | collective-permute-start | bytes 1572872 | tf_op jit(solution)/shard_map/ppermute | solution.py:468
  62.1 13.5 %collective-permute-start.7 = (bf16[128,2048]{1,0:T(8,128)(2,1)S(1)}, bf16[128,2048]{1,0:T(8,128)(2,1)S(1)}, u32[]{:S(2)}, u32[]{:S(2)}) collective-permute-start(bf16[128,2048]{1,0:T(8,128)(2,1)S(1)} %get-tuple-element.75), channel_id=1, source_target_pairs={{0,8},{1,9},{2,10},{3,11},{4,12},{5,13},{6,14},{7,15},{8,16},{9,17... | collective-permute-start | bytes 1572872 | tf_op jit(solution)/shard_map/ppermute | solution.py:468
  62.3 13.2 %collective-permute-start.8 = (bf16[128,2048]{1,0:T(8,128)(2,1)S(1)}, bf16[128,2048]{1,0:T(8,128)(2,1)S(1)}, u32[]{:S(2)}, u32[]{:S(2)}) collective-permute-start(bf16[128,2048]{1,0:T(8,128)(2,1)S(1)} %get-tuple-element.76), channel_id=1, source_target_pairs={{0,24},{1,25},{2,26},{3,27},{4,28},{5,29},{6,30},{7,31},{8,0},{9,1... | collective-permute-start | bytes 1572872 | tf_op jit(solution)/shard_map/ppermute | solution.py:468
  64.7 12.9 %collective-permute-start.9 = (bf16[128,2048]{1,0:T(8,128)(2,1)S(1)}, bf16[128,2048]{1,0:T(8,128)(2,1)}, u32[]{:S(2)}, u32[]{:S(2)}) collective-permute-start(bf16[128,2048]{1,0:T(8,128)(2,1)S(1)} %get-tuple-element.77), channel_id=1, source_target_pairs={{0,2},{1,3},{2,4},{3,5},{4,6},{5,7},{6,0},{7,1},{8,10},{9,11},{10,... | collective-permute-start | bytes 1572872 | tf_op jit(solution)/shard_map/ppermute | solution.py:468
  65.9 32.6 %collective-permute-start.3 = (bf16[128,2048]{1,0:T(8,128)(2,1)}, bf16[128,2048]{1,0:T(8,128)(2,1)}, u32[]{:S(2)}, u32[]{:S(2)}) collective-permute-start(bf16[128,2048]{1,0:T(8,128)(2,1)} %get-tuple-element.61), channel_id=1, source_target_pairs={{0,32},{1,33},{2,34},{3,35},{4,36},{5,37},{6,38},{7,39},{8,40},{9,... | collective-permute-start | bytes 1572872 | tf_op jit(solution)/shard_map/ppermute | solution.py:468
  74.2 1.3 copy-start.11
  74.2 24.4 %collective-permute-start.4 = (bf16[128,2048]{1,0:T(8,128)(2,1)}, bf16[128,2048]{1,0:T(8,128)(2,1)}, u32[]{:S(2)}, u32[]{:S(2)}) collective-permute-start(bf16[128,2048]{1,0:T(8,128)(2,1)} %get-tuple-element.62), channel_id=1, source_target_pairs={{0,96},{1,97},{2,98},{3,99},{4,100},{5,101},{6,102},{7,103},{8,104... | collective-permute-start | bytes 1572872 | tf_op jit(solution)/shard_map/ppermute | solution.py:468
  78.4 21.4 %collective-permute-start.11 = (bf16[128,2048]{1,0:T(8,128)(2,1)}, bf16[128,2048]{1,0:T(8,128)(2,1)S(1)}, u32[]{:S(2)}, u32[]{:S(2)}) collective-permute-start(bf16[128,2048]{1,0:T(8,128)(2,1)} %get-tuple-element.79), channel_id=1, source_target_pairs={{0,24},{1,25},{2,26},{3,27},{4,28},{5,29},{6,30},{7,31},{8,0},{9,1... | collective-permute-start | bytes 1572872 | tf_op jit(solution)/shard_map/ppermute | solution.py:475
  88.6 20.1 %collective-permute-start.12 = (bf16[128,2048]{1,0:T(8,128)(2,1)}, bf16[128,2048]{1,0:T(8,128)(2,1)S(1)}, u32[]{:S(2)}, u32[]{:S(2)}) collective-permute-start(bf16[128,2048]{1,0:T(8,128)(2,1)} %get-tuple-element.80), channel_id=1, source_target_pairs={{0,8},{1,9},{2,10},{3,11},{4,12},{5,13},{6,14},{7,15},{8,16},{9,17... | collective-permute-start | bytes 1572872 | tf_op jit(solution)/shard_map/ppermute | solution.py:475
  89.0 19.7 %collective-permute-start.13 = (bf16[128,2048]{1,0:T(8,128)(2,1)}, bf16[128,2048]{1,0:T(8,128)(2,1)S(1)}, u32[]{:S(2)}, u32[]{:S(2)}) collective-permute-start(bf16[128,2048]{1,0:T(8,128)(2,1)} %get-tuple-element.81), channel_id=1, source_target_pairs={{0,6},{1,7},{2,0},{3,1},{4,2},{5,3},{6,4},{7,5},{8,14},{9,15},{10,... | collective-permute-start | bytes 1572872 | tf_op jit(solution)/shard_map/ppermute | solution.py:475
  98.6 12.6 %collective-permute-start.14 = (bf16[128,2048]{1,0:T(8,128)(2,1)}, bf16[128,2048]{1,0:T(8,128)(2,1)}, u32[]{:S(2)}, u32[]{:S(2)}) collective-permute-start(bf16[128,2048]{1,0:T(8,128)(2,1)} %get-tuple-element.82), channel_id=1, source_target_pairs={{0,2},{1,3},{2,4},{3,5},{4,6},{5,7},{6,0},{7,1},{8,10},{9,11},{10,... | collective-permute-start | bytes 1572872 | tf_op jit(solution)/shard_map/ppermute | solution.py:475
  98.6 13.2 %copy-start.2 = (bf16[512,2048]{1,0:T(8,128)(2,1)S(1)}, bf16[512,2048]{1,0:T(8,128)(2,1)}, u32[]{:S(2)}) copy-start(bf16[512,2048]{1,0:T(8,128)(2,1)} %copy-done.1) | copy-start | bytes 6291460
  98.6 13.2 %copy-start.8 = (s32[1,128]{1,0:T(1,128)S(1)}, s32[1,128]{1,0:T(1,128)}, u32[]{:S(2)}) copy-start(s32[1,128]{1,0:T(1,128)} %copy-done.7) | copy-start | bytes 1540
  99.7 11.4 %collective-permute-start.5 = (bf16[128,2048]{1,0:T(8,128)(2,1)}, bf16[128,2048]{1,0:T(8,128)(2,1)S(1)}, u32[]{:S(2)}, u32[]{:S(2)}) collective-permute-start(bf16[128,2048]{1,0:T(8,128)(2,1)} %get-tuple-element.73), channel_id=1, source_target_pairs={{0,96},{1,97},{2,98},{3,99},{4,100},{5,101},{6,102},{7,103},{8,104... | collective-permute-start | bytes 1572872 | tf_op jit(solution)/shard_map/ppermute | solution.py:475
  99.8 12.0 %collective-permute-start.6 = (bf16[128,2048]{1,0:T(8,128)(2,1)}, bf16[128,2048]{1,0:T(8,128)(2,1)S(1)}, u32[]{:S(2)}, u32[]{:S(2)}) collective-permute-start(bf16[128,2048]{1,0:T(8,128)(2,1)} %get-tuple-element.74), channel_id=1, source_target_pairs={{0,32},{1,33},{2,34},{3,35},{4,36},{5,37},{6,38},{7,39},{8,40},{9,... | collective-permute-start | bytes 1572872 | tf_op jit(solution)/shard_map/ppermute | solution.py:475
  115.6 1.6 copy-start
  117.2 19.2 %copy-start.14 = (f32[64,8]{0,1:T(8,128)S(1)}, f32[64,8]{0,1:T(8,128)}, u32[]{:S(2)}) copy-start(f32[64,8]{0,1:T(8,128)} %param.10) | copy-start | bytes 6148
  117.2 62.1 %copy-start.10 = (bf16[64,2048]{1,0:T(8,128)(2,1)S(1)}, bf16[64,2048]{1,0:T(8,128)(2,1)}, u32[]{:S(2)}) copy-start(bf16[64,2048]{1,0:T(8,128)(2,1)} %tok_ref.1) | copy-start | bytes 786436
  117.2 62.1 %copy-start.15 = (s32[64,8]{0,1:T(8,128)S(1)}, s32[64,8]{0,1:T(8,128)}, u32[]{:S(2)}) copy-start(s32[64,8]{0,1:T(8,128)} %param.9) | copy-start | bytes 6148
  117.2 60.3 %all-to-all-start.3 = ((bf16[128,4,3072]{2,1,0:T(4,128)(2,1)}), bf16[128,4,3072]{2,1,0:T(4,128)(2,1)S(1)}, u32[]{:S(2)}, u32[]{:S(2)}) async-start(bf16[128,4,3072]{2,1,0:T(4,128)(2,1)} %copy-done), calls=%async_computation.3 | async-start | bytes 6291456 | tf_op jit(solution)/shard_map/all_to_all | solution.py:455
  (7 other events, 6.6 us)

commit v3 on v0

--- a/solution.py
+++ b/solution.py
@@ -443,9 +443,9 @@
         lax.ppermute(x, "expert", hop_pairs(axis, step, n)) for x, (axis, step) in zip(sent, DIRS)
     ]
     first = hot_ffn(flags, kept, own, other)
-    first, early = lax.optimization_barrier((first, hopped[:3]))
+    first, early = lax.optimization_barrier((first, hopped[:5]))
     second = hot_ffn(flags, early, own, other)
-    third = hot_ffn(flags, hopped[3:], own, other)
+    third = hot_ffn(flags, hopped[5:], own, other)
     back = [
         lax.ppermute(x, "expert", hop_pairs(axis, -step, n))
         for x, (axis, step) in zip(list(second) + list(third), DIRS)

time: 173 us -> 173 us (level)
  waiting for transfers between devices: 69.9 us -> 75.2 us
  starting transfers between devices: 43.5 us -> 39.1 us
    ppermute x6, waiting for transfers between devices: 5.09 us -> 10.5 us  [relayed(): lax.ppermute(x, 'expert', hop_pairs(axis, -step, n))]
    ppermute x6, starting transfers between devices: 20.8 us -> 16.1 us  [relayed(): lax.ppermute(x, 'expert', hop_pairs(axis, -step, n))]
where the time goes in v3:
time: 173 us; the launch traced here: 172 us
  waiting for transfers between devices  75.2 us (43%)
  starting transfers between devices  39.1 us (23%)
  blocking collectives  29.1 us (17%)
  Pallas kernels  21.6 us (12%)
  local copies, waits for them, and re-layouts  6.21 us (4%)
    all_to_all x2, waiting for transfers between devices, exchange(): return lax.all_to_all(x, 'expert', split_axis=0, concat_axis=0, tiled=True)  40.4 us
    all_to_all x1, blocking collectives, exchange(): return lax.all_to_all(x, 'expert', split_axis=0, concat_axis=0, tiled=True)  29.1 us
    ppermute x6, waiting for transfers between devices, relayed(): lax.ppermute(x, 'expert', hop_pairs(axis, step, n))  24.3 us
    ppermute x6, starting transfers between devices, relayed(): lax.ppermute(x, 'expert', hop_pairs(axis, -step, n))  16.1 us
    all_to_all x2, starting transfers between devices, exchange(): return lax.all_to_all(x, 'expert', split_axis=0, concat_axis=0, tiled=True)  11.4 us
    ppermute x6, waiting for transfers between devices, relayed(): lax.ppermute(x, 'expert', hop_pairs(axis, -step, n))  10.5 us
    ppermute x6, starting transfers between devices, relayed(): lax.ppermute(x, 'expert', hop_pairs(axis, step, n))  9.68 us
    pallas_call x1, Pallas kernels, ffn(): pl.pallas_call(ffn_kernel, in_specs=[VMEM] + [HBM] * 3, out_specs=VMEM, o...  7.78 us
  transfers between devices with their start and end apart: 17, of which 4 were waited for; matrix products, arithmetic and copies ran while one was open for 1% of the time, Pallas kernels for 10%

profile of v3, /device:TPU:1, one launch (start us, length us, event | category | flops | bytes accessed | tf_op | source)
XLA Modules:
  0.0 172.0 jit_solution(15076079712089266055)
XLA Ops:
  0.0 1.4 collective-permute-start
  2.7 4.3 %plan.1 = (bf16[128,4,2048]{2,1,0:T(4,128)(2,1)}, bf16[128,2,2048]{2,1,0:T(2,128)(2,1)S(1)}, s32[64,8]{1,0:T(8,128)S(1)}, s32[1,128]{1,0:T(1,128)S(1)}) custom-call(s32[1]{0:T(128)} %bitcast.10.me_ref, s32[64,8]{1,0:T(8,128)S(1)} %copy.14.ids_ref, bf16[64,2048]{1,0:T(8,128)(2,1)} %tok_ref.1), custom_call_target="tpu_custom_call" | custom-call | tf_op jit(solution)/shard_map/plan/pallas_call | solution.py:146
  7.0 29.1 %all_to_all.24.got_ref = bf16[128,2,2048]{2,1,0:T(2,128)(2,1)S(1)} all-to-all(bf16[128,2,2048]{2,1,0:T(2,128)(2,1)S(1)} %get-tuple-element.61), channel_id=1, replica_groups=mesh['expert'=128] {'expert'}, dimensions={0} | all-to-all | bytes 2097152 | tf_op jit(solution)/shard_map/all_to_all | solution.py:429
  36.1 4.7 %all-to-all-start.3 = ((bf16[128,4,2048]{2,1,0:T(4,128)(2,1)}), bf16[128,4,2048]{2,1,0:T(4,128)(2,1)S(1)}, u32[]{:S(2)}, u32[]{:S(2)}) async-start(bf16[128,4,2048]{2,1,0:T(4,128)(2,1)} %get-tuple-element.63), calls=%async_computation.3 | async-start | bytes 4194304 | tf_op jit(solution)/shard_map/all_to_all | solution.py:429
  40.8 2.7 %spread.1 = (bf16[128,2048]{1,0:T(8,128)(2,1)S(1)}, bf16[128,2048]{1,0:T(8,128)(2,1)S(1)}, bf16[128,2048]{1,0:T(8,128)(2,1)}, bf16[128,2048]{1,0:T(8,128)(2,1)},...) custom-call(s32[128]{0:T(128)S(1)} %bitcast.36, ...), custom_call_target="tpu_custom_call" | custom-call | tf_op jit(solution)/shard_map/spread/pallas_call | solution.py:189
  45.1 1.4 collective-permute-start.4
  46.5 1.3 collective-permute-start.5
  47.8 1.6 collective-permute-start.6
  49.4 1.8 %collective-permute-start.7 = (bf16[128,2048]{1,0:T(8,128)(2,1)}, bf16[128,2048]{1,0:T(8,128)(2,1)}, u32[]{:S(2)}, u32[]{:S(2)}) collective-permute-start(bf16[128,2048]{1,0:T(8,128)(2,1)} %get-tuple-element.77), channel_id=1, source_target_pairs={{0,24},{1,25},{2,26},{3,27},{4,28},{5,29},{6,30},{7,31},{8,0},{9,1... | collective-permute-start | bytes 1572872 | tf_op jit(solution)/shard_map/ppermute | solution.py:443
  51.1 1.2 collective-permute-start.8
  53.1 24.3 %collective-permute-done.4.refs_0_ = bf16[128,2048]{1,0:T(8,128)(2,1)S(1)} collective-permute-done((bf16[128,2048]{1,0:T(8,128)(2,1)}, bf16[128,2048]{1,0:T(8,128)(2,1)S(1)}, u32[]{:S(2)}, u32[]{:S(2)}) %collective-permute-start.4) | collective-permute-done | bytes 524320 | tf_op jit(solution)/shard_map/ppermute | solution.py:443
  77.5 2.4 %collective-permute-start.3 = (bf16[128,2048]{1,0:T(8,128)(2,1)}, bf16[128,2048]{1,0:T(8,128)(2,1)S(1)}, u32[]{:S(2)}, u32[]{:S(2)}) collective-permute-start(bf16[128,2048]{1,0:T(8,128)(2,1)} %get-tuple-element.65), channel_id=1, source_target_pairs={{0,6},{1,7},{2,0},{3,1},{4,2},{5,3},{6,4},{7,5},{8,14},{9,15},{10,... | collective-permute-start | bytes 1572872 | tf_op jit(solution)/shard_map/ppermute | solution.py:443
  79.9 0.8 hot_ffn.5
  80.7 11.5 %collective-permute-start.10 = (bf16[128,2048]{1,0:T(8,128)(2,1)}, bf16[128,2048]{1,0:T(8,128)(2,1)S(1)}, u32[]{:S(2)}, u32[]{:S(2)}) collective-permute-start(bf16[128,2048]{1,0:T(8,128)(2,1)} %get-tuple-element.87), channel_id=1, source_target_pairs={{0,32},{1,33},{2,34},{3,35},{4,36},{5,37},{6,38},{7,39},{8,40},{9,... | collective-permute-start | bytes 1572872 | tf_op jit(solution)/shard_map/ppermute | solution.py:450
  92.2 1.5 collective-permute-start.12
  95.3 7.9 %collective-permute-done.10.refs_3_ = bf16[128,2048]{1,0:T(8,128)(2,1)S(1)} collective-permute-done((bf16[128,2048]{1,0:T(8,128)(2,1)}, bf16[128,2048]{1,0:T(8,128)(2,1)S(1)}, u32[]{:S(2)}, u32[]{:S(2)}) %collective-permute-start.10) | collective-permute-done | bytes 524320 | tf_op jit(solution)/shard_map/ppermute | solution.py:450
  104.0 3.1 %collective-permute-start.14 = (bf16[128,2048]{1,0:T(8,128)(2,1)}, bf16[128,2048]{1,0:T(8,128)(2,1)}, u32[]{:S(2)}, u32[]{:S(2)}) collective-permute-start(bf16[128,2048]{1,0:T(8,128)(2,1)} %hot_ffn.3), channel_id=1, source_target_pairs={{0,2},{1,3},{2,4},{3,5},{4,6},{5,7},{6,0},{7,1},{8,10},{9,11},{10,... | collective-permute-start | bytes 1572872 | tf_op jit(solution)/shard_map/ppermute | solution.py:450
  107.1 7.8 %ffn.1.served_ref = bf16[512,2048]{1,0:T(8,128)(2,1)S(1)} custom-call(bf16[128,4,2048]{2,1,0:T(4,128)(2,1)S(1)} %all-to-all-done.3.x_ref, bf16[1,2048,768]{2,1,0:T(8,128)(2,1)} %refs_5_.1, bf16[1,2048,768]{2,1,0:T(8,128)(2,1)} %refs_6_.1, bf16[1,768,2048]{2,1,0:T(8,128)(2,1)} %refs_7_.1), custom_call_target="tpu_custom_call" | custom-call | flops 4831838208 | bytes 9437184 | tf_op jit(solution)/shard_map/ffn/pallas_call | solution.py:267
  114.9 2.6 %collective-permute-done.14.refs_7_ = bf16[128,2048]{1,0:T(8,128)(2,1)} collective-permute-done((bf16[128,2048]{1,0:T(8,128)(2,1)}, bf16[128,2048]{1,0:T(8,128)(2,1)}, u32[]{:S(2)}, u32[]{:S(2)}) %collective-permute-start.14) | collective-permute-done | bytes 524320 | tf_op jit(solution)/shard_map/ppermute | solution.py:450
  117.5 2.6 %join.1 = bf16[128,4,3072]{2,1,0:T(4,128)(2,1)S(1)} custom-call(s32[128]{0:T(128)S(1)} %bitcast.40, bf16[512,2048]{1,0:T(8,128)(2,1)S(1)} %ffn.1.served_ref, bf16[128,2048]{1,0:T(8,128)(2,1)S(1)} %copy-done.1, bf16[128,2048]{1,0:T(8,128)(2,1)S(1)} %copy-done.2, bf16[128,2048]{1,0:T(8,128)(2,1)} %collective-permute-done.9.refs_2_, ...), custom_call_target="tpu_custom_call" | custom-call | tf_op jit(solution)/shard_map/join/pallas_call | solution.py:374
  120.1 1.6 copy-done
  121.8 6.7 %all-to-all-start.4 = ((bf16[128,4,3072]{2,1,0:T(4,128)(2,1)}), bf16[128,4,3072]{2,1,0:T(4,128)(2,1)S(1)}, u32[]{:S(2)}, u32[]{:S(2)}) async-start(bf16[128,4,3072]{2,1,0:T(4,128)(2,1)} %copy-done), calls=%async_computation.4 | async-start | bytes 6291456 | tf_op jit(solution)/shard_map/all_to_all | solution.py:429
  129.8 40.4 %all-to-all-done.4.ans_ref = bf16[128,4,3072]{2,1,0:T(4,128)(2,1)S(1)} async-done(((bf16[128,4,3072]{2,1,0:T(4,128)(2,1)}), bf16[128,4,3072]{2,1,0:T(4,128)(2,1)S(1)}, u32[]{:S(2)}, u32[]{:S(2)}) %all-to-all-start.4) | async-done | bytes 3145760 | tf_op jit(solution)/shard_map/all_to_all | solution.py:429
  170.1 1.8 %mix.1 = bf16[64,2048]{1,0:T(8,128)(2,1)} custom-call(f32[64,8]{1,0:T(8,128)S(1)} %copy.15.score_ref, s32[64,8]{1,0:T(8,128)S(1)} %get-tuple-element.60.slot_ref, bf16[128,4,3072]{2,1,0:T(4,128)(2,1)S(1)} %all-to-all-done.4.ans_ref), custom_call_target="tpu_custom_call" | custom-call | tf_op jit(solution)/shard_map/mix/pallas_call | solution.py:418
  (51 shorter events, 6.8 us)
Async XLA Ops:
  0.0 36.1 %collective-permute-start = (bf16[1,2048,768]{2,1,0:T(8,128)(2,1)}, bf16[1,2048,768]{2,1,0:T(8,128)(2,1)}, u32[]{:S(2)}, u32[]{:S(2)}) collective-permute-start(bf16[1,2048,768]{2,1,0:T(8,128)(2,1)} %refs_5_.1), channel_id=1, source_target_pairs={{0,1},{1,0},{2,3},{3,2},{4,5},{5,4},{6,7},{7,6},{8,9},{9,8},{10,11... | collective-permute-start | bytes 9437192 | tf_op jit(solution)/shard_map/ppermute | solution.py:437
  1.4 34.7 %collective-permute-start.1 = (bf16[1,2048,768]{2,1,0:T(8,128)(2,1)}, bf16[1,2048,768]{2,1,0:T(8,128)(2,1)}, u32[]{:S(2)}, u32[]{:S(2)}) collective-permute-start(bf16[1,2048,768]{2,1,0:T(8,128)(2,1)} %refs_6_.1), channel_id=1, source_target_pairs={{0,1},{1,0},{2,3},{3,2},{4,5},{5,4},{6,7},{7,6},{8,9},{9,8},{10,11... | collective-permute-start | bytes 9437192 | tf_op jit(solution)/shard_map/ppermute | solution.py:437
  1.4 34.7 %collective-permute-start.2 = (bf16[1,768,2048]{2,1,0:T(8,128)(2,1)}, bf16[1,768,2048]{2,1,0:T(8,128)(2,1)}, u32[]{:S(2)}, u32[]{:S(2)}) collective-permute-start(bf16[1,768,2048]{2,1,0:T(8,128)(2,1)} %refs_7_.1), channel_id=1, source_target_pairs={{0,1},{1,0},{2,3},{3,2},{4,5},{5,4},{6,7},{7,6},{8,9},{9,8},{10,11... | collective-permute-start | bytes 9437192 | tf_op jit(solution)/shard_map/ppermute | solution.py:437
  7.0 45.3 %copy-start.7 = (s32[1,128]{1,0:T(1,128)}, s32[1,128]{1,0:T(1,128)S(1)}, u32[]{:S(2)}) copy-start(s32[1,128]{1,0:T(1,128)S(1)} %get-tuple-element.59) | copy-start | bytes 1540
  36.1 71.0 %all-to-all-start.3 = ((bf16[128,4,2048]{2,1,0:T(4,128)(2,1)}), bf16[128,4,2048]{2,1,0:T(4,128)(2,1)S(1)}, u32[]{:S(2)}, u32[]{:S(2)}) async-start(bf16[128,4,2048]{2,1,0:T(4,128)(2,1)} %get-tuple-element.63), calls=%async_computation.3 | async-start | bytes 4194304 | tf_op jit(solution)/shard_map/all_to_all | solution.py:429
  45.1 32.4 %collective-permute-start.4 = (bf16[128,2048]{1,0:T(8,128)(2,1)}, bf16[128,2048]{1,0:T(8,128)(2,1)S(1)}, u32[]{:S(2)}, u32[]{:S(2)}) collective-permute-start(bf16[128,2048]{1,0:T(8,128)(2,1)} %get-tuple-element.74), channel_id=1, source_target_pairs={{0,32},{1,33},{2,34},{3,35},{4,36},{5,37},{6,38},{7,39},{8,40},{9,... | collective-permute-start | bytes 1572872 | tf_op jit(solution)/shard_map/ppermute | solution.py:443
  46.5 33.4 %collective-permute-start.5 = (bf16[128,2048]{1,0:T(8,128)(2,1)}, bf16[128,2048]{1,0:T(8,128)(2,1)}, u32[]{:S(2)}, u32[]{:S(2)}) collective-permute-start(bf16[128,2048]{1,0:T(8,128)(2,1)} %get-tuple-element.75), channel_id=1, source_target_pairs={{0,96},{1,97},{2,98},{3,99},{4,100},{5,101},{6,102},{7,103},{8,104... | collective-permute-start | bytes 1572872 | tf_op jit(solution)/shard_map/ppermute | solution.py:443
  47.8 32.1 %collective-permute-start.6 = (bf16[128,2048]{1,0:T(8,128)(2,1)}, bf16[128,2048]{1,0:T(8,128)(2,1)}, u32[]{:S(2)}, u32[]{:S(2)}) collective-permute-start(bf16[128,2048]{1,0:T(8,128)(2,1)} %get-tuple-element.76), channel_id=1, source_target_pairs={{0,8},{1,9},{2,10},{3,11},{4,12},{5,13},{6,14},{7,15},{8,16},{9,17... | collective-permute-start | bytes 1572872 | tf_op jit(solution)/shard_map/ppermute | solution.py:443
  49.4 30.5 %collective-permute-start.7 = (bf16[128,2048]{1,0:T(8,128)(2,1)}, bf16[128,2048]{1,0:T(8,128)(2,1)}, u32[]{:S(2)}, u32[]{:S(2)}) collective-permute-start(bf16[128,2048]{1,0:T(8,128)(2,1)} %get-tuple-element.77), channel_id=1, source_target_pairs={{0,24},{1,25},{2,26},{3,27},{4,28},{5,29},{6,30},{7,31},{8,0},{9,1... | collective-permute-start | bytes 1572872 | tf_op jit(solution)/shard_map/ppermute | solution.py:443
  51.1 28.8 %collective-permute-start.8 = (bf16[128,2048]{1,0:T(8,128)(2,1)S(1)}, bf16[128,2048]{1,0:T(8,128)(2,1)}, u32[]{:S(2)}, u32[]{:S(2)}) collective-permute-start(bf16[128,2048]{1,0:T(8,128)(2,1)S(1)} %get-tuple-element.78), channel_id=1, source_target_pairs={{0,2},{1,3},{2,4},{3,5},{4,6},{5,7},{6,0},{7,1},{8,10},{9,11},{10,... | collective-permute-start | bytes 1572872 | tf_op jit(solution)/shard_map/ppermute | solution.py:443
  77.5 16.2 %collective-permute-start.3 = (bf16[128,2048]{1,0:T(8,128)(2,1)}, bf16[128,2048]{1,0:T(8,128)(2,1)S(1)}, u32[]{:S(2)}, u32[]{:S(2)}) collective-permute-start(bf16[128,2048]{1,0:T(8,128)(2,1)} %get-tuple-element.65), channel_id=1, source_target_pairs={{0,6},{1,7},{2,0},{3,1},{4,2},{5,3},{6,4},{7,5},{8,14},{9,15},{10,... | collective-permute-start | bytes 1572872 | tf_op jit(solution)/shard_map/ppermute | solution.py:443
  80.7 22.4 %collective-permute-start.10 = (bf16[128,2048]{1,0:T(8,128)(2,1)}, bf16[128,2048]{1,0:T(8,128)(2,1)S(1)}, u32[]{:S(2)}, u32[]{:S(2)}) collective-permute-start(bf16[128,2048]{1,0:T(8,128)(2,1)} %get-tuple-element.87), channel_id=1, source_target_pairs={{0,32},{1,33},{2,34},{3,35},{4,36},{5,37},{6,38},{7,39},{8,40},{9,... | collective-permute-start | bytes 1572872 | tf_op jit(solution)/shard_map/ppermute | solution.py:450
  92.2 22.7 %collective-permute-start.11 = (bf16[128,2048]{1,0:T(8,128)(2,1)}, bf16[128,2048]{1,0:T(8,128)(2,1)}, u32[]{:S(2)}, u32[]{:S(2)}) collective-permute-start(bf16[128,2048]{1,0:T(8,128)(2,1)} %get-tuple-element.88), channel_id=1, source_target_pairs={{0,24},{1,25},{2,26},{3,27},{4,28},{5,29},{6,30},{7,31},{8,0},{9,1... | collective-permute-start | bytes 1572872 | tf_op jit(solution)/shard_map/ppermute | solution.py:450
  92.2 22.7 %collective-permute-start.12 = (bf16[128,2048]{1,0:T(8,128)(2,1)}, bf16[128,2048]{1,0:T(8,128)(2,1)}, u32[]{:S(2)}, u32[]{:S(2)}) collective-permute-start(bf16[128,2048]{1,0:T(8,128)(2,1)} %get-tuple-element.89), channel_id=1, source_target_pairs={{0,8},{1,9},{2,10},{3,11},{4,12},{5,13},{6,14},{7,15},{8,16},{9,17... | collective-permute-start | bytes 1572872 | tf_op jit(solution)/shard_map/ppermute | solution.py:450
  93.7 21.2 %collective-permute-start.13 = (bf16[128,2048]{1,0:T(8,128)(2,1)}, bf16[128,2048]{1,0:T(8,128)(2,1)}, u32[]{:S(2)}, u32[]{:S(2)}) collective-permute-start(bf16[128,2048]{1,0:T(8,128)(2,1)} %get-tuple-element.90), channel_id=1, source_target_pairs={{0,6},{1,7},{2,0},{3,1},{4,2},{5,3},{6,4},{7,5},{8,14},{9,15},{10,... | collective-permute-start | bytes 1572872 | tf_op jit(solution)/shard_map/ppermute | solution.py:450
  93.7 21.2 %collective-permute-start.9 = (bf16[128,2048]{1,0:T(8,128)(2,1)}, bf16[128,2048]{1,0:T(8,128)(2,1)}, u32[]{:S(2)}, u32[]{:S(2)}) collective-permute-start(bf16[128,2048]{1,0:T(8,128)(2,1)} %get-tuple-element.86), channel_id=1, source_target_pairs={{0,96},{1,97},{2,98},{3,99},{4,100},{5,101},{6,102},{7,103},{8,104... | collective-permute-start | bytes 1572872 | tf_op jit(solution)/shard_map/ppermute | solution.py:450
  95.3 22.2 %copy-start.1 = (bf16[128,2048]{1,0:T(8,128)(2,1)S(1)}, bf16[128,2048]{1,0:T(8,128)(2,1)}, u32[]{:S(2)}) copy-start(bf16[128,2048]{1,0:T(8,128)(2,1)} %get-tuple-element.79.refs_0_) | copy-start | bytes 1572868
  95.3 22.2 %copy-start.2 = (bf16[128,2048]{1,0:T(8,128)(2,1)S(1)}, bf16[128,2048]{1,0:T(8,128)(2,1)}, u32[]{:S(2)}) copy-start(bf16[128,2048]{1,0:T(8,128)(2,1)} %get-tuple-element.80.refs_1_) | copy-start | bytes 1572868
  95.3 22.2 %copy-start.8 = (s32[1,128]{1,0:T(1,128)S(1)}, s32[1,128]{1,0:T(1,128)}, u32[]{:S(2)}) copy-start(s32[1,128]{1,0:T(1,128)} %copy-done.7) | copy-start | bytes 1540
  104.0 13.5 %collective-permute-start.14 = (bf16[128,2048]{1,0:T(8,128)(2,1)}, bf16[128,2048]{1,0:T(8,128)(2,1)}, u32[]{:S(2)}, u32[]{:S(2)}) collective-permute-start(bf16[128,2048]{1,0:T(8,128)(2,1)} %hot_ffn.3), channel_id=1, source_target_pairs={{0,2},{1,3},{2,4},{3,5},{4,6},{5,7},{6,0},{7,1},{8,10},{9,11},{10,... | collective-permute-start | bytes 1572872 | tf_op jit(solution)/shard_map/ppermute | solution.py:450
  107.1 10.4 %copy-start.4 = (bf16[128,2048]{1,0:T(8,128)(2,1)S(1)}, bf16[128,2048]{1,0:T(8,128)(2,1)}, u32[]{:S(2)}) copy-start(bf16[128,2048]{1,0:T(8,128)(2,1)} %copy-done.3) | copy-start | bytes 1572868
  121.7 50.2 %copy-start.10 = (bf16[64,2048]{1,0:T(8,128)(2,1)S(1)}, bf16[64,2048]{1,0:T(8,128)(2,1)}, u32[]{:S(2)}) copy-start(bf16[64,2048]{1,0:T(8,128)(2,1)} %tok_ref.1) | copy-start | bytes 786436
  121.7 50.2 %copy-start.13 = (s32[64,8]{0,1:T(8,128)S(1)}, s32[64,8]{0,1:T(8,128)}, u32[]{:S(2)}) copy-start(s32[64,8]{0,1:T(8,128)} %param.9) | copy-start | bytes 6148
  121.8 48.4 %all-to-all-start.4 = ((bf16[128,4,3072]{2,1,0:T(4,128)(2,1)}), bf16[128,4,3072]{2,1,0:T(4,128)(2,1)S(1)}, u32[]{:S(2)}, u32[]{:S(2)}) async-start(bf16[128,4,3072]{2,1,0:T(4,128)(2,1)} %copy-done), calls=%async_computation.4 | async-start | bytes 6291456 | tf_op jit(solution)/shard_map/all_to_all | solution.py:429
  (7 other events, 14.6 us)
